TPU v7x, 32 devices: a whole 2x2x4 slice. The times are simulated.
32 devices in a mesh: dp: 16 (over z, y, x), group: 2 (over core).
Axes of the slice: x: 2, y: 2, z: 4, core: 2. Of those that a mesh axis runs over, the one named last changes fastest.
Arguments:
- embeddings: bfloat16 [32768, 1024], P('dp', 'group'), may hold values from -6 to 6
- assignment: int32 [32768], P('dp'), may hold values from -1 to 65535, as said below
- prev_counts: int32 [65536], P('dp'), may hold values from 1 to 8
- old_centroids: float32 [65536, 1024], P('dp', 'group'), may hold values from -4 to 4
- block_owner: int32 [1024], replicated, may hold values from 0 to 15, as said below
Outputs:
- new_centroids: float32 [65536, 1024], P('dp', 'group')
- max_sim: float32 [32768], P('dp')
Inputs may be any that keep to these rules, and one draw needn't show every extreme that they name: `block_owner`: every owner owns exactly 64 blocks. `assignment`: -1 marks a padding document. On each index of dp, at most 256 documents belong to clusters of blocks owned by one index of dp, and some owner receives exactly 256 from every index of dp.
All inputs are finite; a program needn't handle non-finite values.
Results may differ from a plain program's by a relative error of at most 0.0003.
Values may be sent and summed in bfloat16 or wider, within the bound.
A program may use at most 128 MiB of HBM per device.

v0:
```python
import jax
import jax.numpy as jnp
from jax import lax
from jax.sharding import PartitionSpec as P

D = 1024
CB = 64


def on_device(embeddings, assignment, prev_counts, old_centroids, block_owner):
    n_dp = lax.axis_size("dp")
    n_grp = lax.axis_size("group")
    grp_index = lax.axis_index("group")
    doc_rows, slice_width = embeddings.shape
    cap = 2 * doc_rows // n_dp
    slots = n_dp * cap
    share = slots // n_grp
    owned = old_centroids.shape[0]
    owner_hot = (block_owner[:, None] == jnp.arange(n_dp, dtype=jnp.int32)[None, :]).astype(
        jnp.int32
    )
    block_rank = jnp.sum((jnp.cumsum(owner_hot, axis=0) - owner_hot) * owner_hot, axis=1)
    valid = assignment >= 0
    safe = jnp.maximum(assignment, 0)
    dest = block_owner[safe // CB]
    dest_hot = (
        (dest[:, None] == jnp.arange(n_dp, dtype=jnp.int32)[None, :]) & valid[:, None]
    ).astype(jnp.int32)
    order_in = jnp.sum((jnp.cumsum(dest_hot, axis=0) - dest_hot) * dest_hot, axis=1)
    slot = jnp.where(valid, dest * cap + order_in, slots)
    source_row = (
        jnp.full((slots + 1,), doc_rows, jnp.int32)
        .at[slot]
        .set(jnp.arange(doc_rows, dtype=jnp.int32))[:slots]
    )
    ids_pad = jnp.concatenate([assignment, jnp.full((1,), -1, jnp.int32)])
    send_ids = ids_pad[source_row].reshape(n_dp, cap)
    full_rows = lax.all_gather(embeddings, "group", axis=1, tiled=True)
    padded = jnp.concatenate([full_rows, jnp.zeros((1, D), full_rows.dtype)], axis=0)
    outgoing = padded[source_row].reshape(n_dp, cap, D)
    got_rows, got_ids = (
        lax.all_to_all(outgoing, "dp", split_axis=0, concat_axis=0, tiled=True),
        lax.all_to_all(send_ids, "dp", split_axis=0, concat_axis=0, tiled=True),
    )
    got_rows = got_rows.reshape(slots, D)
    got_ids = got_ids.reshape(slots)
    features = lax.dynamic_slice_in_dim(got_rows, grp_index * slice_width, slice_width, 1)
    own_rows = lax.dynamic_slice_in_dim(got_rows, grp_index * share, share, 0)
    gram = lax.dot_general(
        own_rows, got_rows, (((1,), (1,)), ((), ())), preferred_element_type=jnp.float32
    )
    squares = jnp.sum(jnp.square(got_rows.astype(jnp.float32)), axis=1)
    inverse = lax.rsqrt(squares + 1e-06)
    own_ids = lax.dynamic_slice_in_dim(got_ids, grp_index * share, share, 0)
    own_inverse = lax.dynamic_slice_in_dim(inverse, grp_index * share, share, 0)
    cosine = gram * own_inverse[:, None] * inverse[None, :]
    row_index = grp_index * share + jnp.arange(share, dtype=jnp.int32)
    same = (own_ids[:, None] == got_ids[None, :]) & (own_ids[:, None] >= 0)
    same = same & (row_index[:, None] != jnp.arange(slots, dtype=jnp.int32)[None, :])
    best = jnp.max(jnp.where(same, cosine, jnp.float32(-1.0)), axis=1)
    every_best = lax.all_gather(best, "group", axis=0, tiled=True)
    returned = lax.all_to_all(
        every_best.reshape(n_dp, cap), "dp", split_axis=0, concat_axis=0, tiled=True
    )
    returned = jnp.concatenate([returned.reshape(slots), jnp.full((1,), -1.0, jnp.float32)])
    max_sim = returned[slot]
    local_id = jnp.maximum(got_ids, 0)
    position = block_rank[local_id // CB] * CB + local_id % CB
    position = jnp.where(got_ids >= 0, position, owned)
    onehot = (jnp.arange(owned, dtype=jnp.int32)[:, None] == position[None, :]).astype(jnp.bfloat16)
    sums = jnp.dot(onehot, features, preferred_element_type=jnp.float32)
    counts = jnp.sum(onehot, axis=1, dtype=jnp.float32)
    prev = prev_counts.astype(jnp.float32)
    new_centroids = (prev[:, None] * old_centroids + sums) / (prev + counts)[:, None]
    return (new_centroids, max_sim)


def solution(mesh):
    return jax.shard_map(
        on_device,
        mesh=mesh,
        in_specs=(P("dp", "group"), P("dp"), P("dp"), P("dp", "group"), P()),
        out_specs=(P("dp", "group"), P("dp")),
        check_vma=False,
    )
```

profile of v0, /device:TPU:0, one launch (start us, length us, event | category | flops | bytes accessed | tf_op | source)
XLA Modules:
  0.0 404.6 jit_solution(15551924638866550384)
XLA Ops:
  7.2 0.0 copy-start.1
  7.2 0.0 all-gather.2.cloned.1.call-start
  7.2 0.7 all-gather.2.cloned.1.call-update
  7.9 0.7 fusion.23
  8.6 10.2 %gather_fusion = s32[2048]{0:T(1024)S(1)} fusion(s32[1024]{0:T(1024)} %param.9, s32[2048]{0:T(1024)S(1)} %fusion.23), kind=kCustom, calls=%fused_computation | custom fusion | bytes 24576 | tf_op jit(solution)/shard_map/gather | solution.py:25
  18.9 0.0 copy-done.1
  18.9 4.5 %reduce-window.14 = s32[16,16,128]{2,1,0:T(8,128)S(1)} reduce-window(s32[16,16,128]{2,1,0:T(8,128)S(1)} %fusion.11, s32[]{:T(128)} %constant.71.clone.1), window={size=1x1x128 pad=0_0x0_0x127_0}, to_apply=%region_0.0 | reduce-window | flops 4161536 | bytes 262148 | tf_op jit(solution)/shard_map/reduce-window
  23.5 0.4 slice_reduce_fusion
  23.9 0.2 reduce-window.15
  24.1 0.1 broadcast_add_fusion
  24.2 0.1 fusion.8
  24.3 8.1 %scatter_custom_fusion = s32[4097]{0:T(1024)S(1)} fusion(s32[2048]{0:T(1024)S(1)} %get-tuple-element.3, s32[2048]{0:T(1024)S(1)} %iota.30, s32[]{:T(128)} %constant.70.clone.1), kind=kCustom, calls=%fused_computation.57 | custom fusion | bytes 16392 | tf_op jit(solution)/shard_map/scatter | solution.py:34
  32.4 40.5 %gather_fusion.1 = s32[4096]{0:T(1024)} fusion(s32[2049]{0:T(1024)S(1)} %pad_add_fusion, s32[4096]{0:T(1024)S(1)} %fusion.18), kind=kCustom, calls=%fused_computation.1 | custom fusion | bytes 49152 | tf_op jit(solution)/shard_map/gather | solution.py:37
  72.9 8.3 %all-to-all-start = ((s32[16,1,256]{2,1,0:T(1,128)}), s32[16,1,256]{2,1,0:T(1,128)S(1)}, u32[]{:S(2)}, u32[]{:S(2)}) async-start(s32[16,1,256]{2,1,0:T(1,128)} %bitcast.3), calls=%async_computation | async-start | bytes 32768 | tf_op jit(solution)/shard_map/all_to_all | solution.py:43
  81.2 0.0 all-gather.2.cloned.1.call-done
  81.3 4.6 %concatenate.10 = bf16[2049,1024]{1,0:T(8,128)(2,1)} pad(bf16[2048,1024]{1,0:T(8,128)(2,1)} %all-gather.2.cloned.1.call-done, bf16[]{:T(256)} %constant.82.clone.1), padding=0_1x0_0 | pad | bytes 8390658 | tf_op jit(solution)/shard_map/concatenate | solution.py:39
  85.8 23.5 %gather_fusion.3 = bf16[4096,1024]{1,0:T(8,128)(2,1)} fusion(bf16[2049,1024]{1,0:T(8,128)(2,1)} %concatenate.10, s32[4096]{0:T(1024)S(1)} %fusion.18), kind=kCustom, calls=%fused_computation.3 | custom fusion | bytes 16793600 | tf_op jit(solution)/shard_map/gather | solution.py:40
  109.3 0.0 all-to-all-done
  109.3 0.0 copy-start
  109.3 0.0 copy-start.2
  109.3 7.1 %all-to-all-start.1 = ((bf16[16,256,1024]{2,1,0:T(8,128)(2,1)}), bf16[16,256,1024]{2,1,0:T(8,128)(2,1)}, u32[]{:S(2)}, u32[]{:S(2)}) async-start(bf16[16,256,1024]{2,1,0:T(8,128)(2,1)} %bitcast.62), calls=%async_computation.1 | async-start | bytes 16777216 | tf_op jit(solution)/shard_map/all_to_all | solution.py:42
  116.5 0.0 copy-done
  116.5 4.5 %reduce-window.16 = s32[16,8,128]{2,1,0:T(8,128)S(1)} reduce-window(s32[16,8,128]{2,1,0:T(8,128)S(1)} %fusion.15, s32[]{:T(128)} %constant.71.clone.1), window={size=1x1x128 pad=0_0x0_0x127_0}, to_apply=%region_4.5 | reduce-window | flops 2080768 | bytes 131076 | tf_op jit(solution)/shard_map/reduce-window.2
  121.0 0.1 slice.33
  121.1 0.1 copy.17
  121.3 0.1 copy.18
  121.3 0.0 copy-done.2
  121.4 0.1 broadcast_add_fusion.1
  121.6 16.7 %gather_fusion.2 = s32[4096]{0:T(1024)S(1)} fusion(s32[1024]{0:T(1024)S(1)} %fusion.14, s32[4096]{0:T(1024)S(1)} %broadcast_clamp_fusion), kind=kCustom, calls=%fused_computation.2 | custom fusion | bytes 49152 | tf_op jit(solution)/shard_map/gather | solution.py:68
  138.4 10.0 %convert_reduce_fusion = f32[4096]{0:T(1024)S(1)} fusion(s32[4096]{0:T(1024)S(1)} %fusion.17), kind=kLoop, calls=%fused_computation.6 | loop fusion | flops 67104768 | bytes 32768 | tf_op jit(solution)/shard_map/reduce_sum | solution.py:72
  148.4 123.4 %all-to-all-done.1 = bf16[16,256,1024]{2,1,0:T(8,128)(2,1)} async-done(((bf16[16,256,1024]{2,1,0:T(8,128)(2,1)}), bf16[16,256,1024]{2,1,0:T(8,128)(2,1)}, u32[]{:S(2)}, u32[]{:S(2)}) %all-to-all-start.1) | async-done | bytes 8388640 | tf_op jit(solution)/shard_map/all_to_all | solution.py:42
  271.7 5.1 %multiply_reduce_fusion = f32[16,256]{1,0:T(8,128)S(1)} fusion(bf16[16,256,1024]{2,1,0:T(8,128)(2,1)} %all-to-all-done.1), kind=kLoop, calls=%fused_computation.14 | loop fusion | flops 12578816 | bytes 8404992 | tf_op jit(solution)/shard_map/reduce_sum | solution.py:52
  276.9 28.9 %select_reduce_fusion = f32[2048]{0:T(1024)S(1)} fusion(bf16[4096,1024]{1,0:T(8,128)(2,1)} %bitcast.10, f32[4096]{0:T(1024)S(1)} %bitcast.74, f32[2048]{0:T(1024)S(1)} %dynamic_slice.15, s32[2048]{0:T(1024)S(1)} %iota_add_fusion, s32[4096]{0:T(1024)S(1)} %bitcast.66, s32[2048]{0:T(1024)S(1)} %get-tuple-element.5, pred[2048]{0:T(1024)(128)(4,1)S(1)} %get-tuple-element.4, ...), kind=kOutput, calls=%fused_computation.10 | convolution fusion | flops 17246976000 | bytes 12650500 | tf_op jit(solution)/shard_map/dot_general | solution.py:49
  305.8 1.9 all_gather.7
  307.7 39.7 %all-to-all-start.2 = ((f32[16,1,256]{2,1,0:T(1,128)}), f32[16,1,256]{2,1,0:T(1,128)S(1)}, u32[]{:S(2)}, u32[]{:S(2)}) async-start(f32[16,1,256]{2,1,0:T(1,128)} %bitcast.11), calls=%async_computation.2 | async-start | bytes 32768 | tf_op jit(solution)/shard_map/all_to_all | solution.py:62
  347.4 29.8 %add_divide_fusion = f32[4096,512]{1,0:T(8,128)} fusion(f32[4096,512]{1,0:T(8,128)} %param.8, s32[4096]{0:T(1024)S(1)} %fusion.17, f32[4096]{0:T(1024)S(1)} %convert_add_fusion, bf16[4096,1024]{1,0:T(8,128)(2,1)} %bitcast.10, s32[]{:T(128)S(6)} %select_n.82, f32[4096]{0:T(1024)S(1)} %convert_element_type.27), kind=kOutput, calls=%fused_computation.15 | convolution fusion | flops 17202937856 | bytes 21020676 | tf_op jit(solution)/shard_map/dot_general | solution.py:71
  377.2 0.0 all-to-all-done.2
  377.2 20.5 %gather_fusion.4 = f32[2048]{0:T(1024)} fusion(f32[4097]{0:T(1024)S(1)} %pad_maximum_fusion, s32[2048]{0:T(1024)S(1)} %get-tuple-element.2), kind=kCustom, calls=%fused_computation.4 | custom fusion | bytes 24576 | tf_op jit(solution)/shard_map/gather | solution.py:66
  (26 shorter events, 0.3 us)
Async XLA Ops:
  7.2 11.7 %copy-start.1 = (s32[2048]{0:T(1024)S(1)}, s32[2048]{0:T(1024)}, u32[]{:S(2)}) copy-start(s32[2048]{0:T(1024)} %param.6) | copy-start | bytes 24580
  7.2 74.1 %all-gather.2.cloned.1.call-start = ((), (), s32[]{:S(2)}) async-start(), calls=%async_computation.3 | async-start | bytes 6291456 | tf_op jit(solution)/shard_map/all_gather | solution.py:38
  72.9 36.4 %all-to-all-start = ((s32[16,1,256]{2,1,0:T(1,128)}), s32[16,1,256]{2,1,0:T(1,128)S(1)}, u32[]{:S(2)}, u32[]{:S(2)}) async-start(s32[16,1,256]{2,1,0:T(1,128)} %bitcast.3), calls=%async_computation | async-start | bytes 32768 | tf_op jit(solution)/shard_map/all_to_all | solution.py:43
  109.3 7.1 %copy-start = (s32[1024]{0:T(1024)S(1)}, s32[1024]{0:T(1024)}, u32[]{:S(2)}) copy-start(s32[1024]{0:T(1024)} %param.9) | copy-start | bytes 12292
  109.3 12.0 %copy-start.2 = (s32[4096]{0:T(1024)S(1)}, s32[4096]{0:T(1024)}, u32[]{:S(2)}) copy-start(s32[4096]{0:T(1024)} %param.7) | copy-start | bytes 49156
  109.3 162.4 %all-to-all-start.1 = ((bf16[16,256,1024]{2,1,0:T(8,128)(2,1)}), bf16[16,256,1024]{2,1,0:T(8,128)(2,1)}, u32[]{:S(2)}, u32[]{:S(2)}) async-start(bf16[16,256,1024]{2,1,0:T(8,128)(2,1)} %bitcast.62), calls=%async_computation.1 | async-start | bytes 16777216 | tf_op jit(solution)/shard_map/all_to_all | solution.py:42
  307.7 69.5 %all-to-all-start.2 = ((f32[16,1,256]{2,1,0:T(1,128)}), f32[16,1,256]{2,1,0:T(1,128)S(1)}, u32[]{:S(2)}, u32[]{:S(2)}) async-start(f32[16,1,256]{2,1,0:T(1,128)} %bitcast.11), calls=%async_computation.2 | async-start | bytes 32768 | tf_op jit(solution)/shard_map/all_to_all | solution.py:62
Sparse Core Ops, SparseCore 0:
  9.6 16.3 all-gather.1
where the time goes:
time: 405 us
  local copies, waits for them, and re-layouts  125 us (31%)
  waiting for transfers between devices  124 us (31%)
  matrix products  58.6 us (14%)
  starting transfers between devices  55.2 us (14%)
  other arithmetic  25.5 us (6%)
  between operations  14.3 us (4%)
    all_to_all x1, waiting for transfers between devices, on_device(): lax.all_to_all(outgoing, 'dp', split_axis=0, concat_axis=0, tiled=True)  123 us
    gather x1, local copies, waits for them, and re-layouts, on_device(): send_ids = ids_pad[source_row].reshape(n_dp, cap)  40.5 us
    all_to_all x1, starting transfers between devices, on_device(): lax.all_to_all(every_best.reshape(n_dp, cap), 'dp', split_axis=0, concat_...  39.7 us
    dot_general x1, matrix products, on_device(): sums = jnp.dot(onehot, features, preferred_element_type=jnp.float32)  29.8 us
    dot_general x1, matrix products, on_device(): lax.dot_general(own_rows, got_rows, (((1,), (1,)), ((), ())), preferred_e...  28.9 us
    gather x1, local copies, waits for them, and re-layouts, on_device(): outgoing = padded[source_row].reshape(n_dp, cap, D)  23.5 us
    gather x1, local copies, waits for them, and re-layouts, on_device(): max_sim = returned[slot]  20.5 us
    gather x1, local copies, waits for them, and re-layouts, on_device(): position = block_rank[local_id // CB] * CB + local_id % CB  16.7 us
  transfers between devices with their start and end apart: 4, of which 1 were waited for; matrix products, arithmetic and copies ran while one was open for 38% of the time, Pallas kernels for 0%

commit v1 on v0

v1 whole, which is shorter than its diff:
```python
import jax
import jax.numpy as jnp
from jax import lax
from jax.experimental import pallas as pl
from jax.experimental.pallas import tpu as pltpu
from jax.sharding import PartitionSpec as P

CB = 64
CHUNKS = 2
NEG = -3.0e38
BF = jnp.bfloat16


def gram_kernel(diagonal, own_ref, all_ref, pos_i, id_i, pos_j, id_j, inv_j, out_ref, best):
    j = pl.program_id(1)

    @pl.when(j == 0)
    def _():
        best[...] = jnp.full_like(best, NEG)

    gram = None
    for part in range(own_ref.shape[0]):
        term = lax.dot_general(
            own_ref[part], all_ref[part], (((1,), (1,)), ((), ())),
            preferred_element_type=jnp.float32,
        )
        gram = term if gram is None else gram + term
    same = pos_i[...] == pos_j[...]
    if diagonal:
        same = same & (id_i[...] != id_j[...])
    value = jnp.where(same, gram * inv_j[...], NEG)
    top = best[...]
    for lane in range(0, value.shape[1], 128):
        top = jnp.maximum(top, value[:, lane : lane + 128])
    best[...] = top

    @pl.when(j == pl.num_programs(1) - 1)
    def _():
        out_ref[...] = jnp.max(best[...], axis=1, keepdims=True)


def gram_best(diagonal, own, every, pos_i, id_i, pos_j, id_j, inv_j):
    parts, rows, half = own.shape
    cols = every.shape[1]
    ti, tj = min(512, rows), min(512, cols)
    column = pl.BlockSpec((ti, 1), lambda i, j: (i, 0))
    line = pl.BlockSpec((1, tj), lambda i, j: (0, j))
    out = pl.pallas_call(
        lambda *refs: gram_kernel(diagonal, *refs),
        grid=(rows // ti, cols // tj),
        in_specs=[
            pl.BlockSpec((parts, ti, half), lambda i, j: (0, i, 0)),
            pl.BlockSpec((parts, tj, half), lambda i, j: (0, j, 0)),
            column, column, line, line, line,
        ],
        out_specs=column,
        out_shape=jax.ShapeDtypeStruct((rows, 1), jnp.float32),
        scratch_shapes=[pltpu.VMEM((ti, 128), jnp.float32)],
        compiler_params=pltpu.CompilerParams(vmem_limit_bytes=32 * 1024 * 1024),
        cost_estimate=pl.CostEstimate(
            flops=2 * rows * cols * parts * half,
            bytes_accessed=2 * parts * half * (rows + cols * (rows // ti)),
            transcendentals=0,
        ),
    )(own, every, pos_i[:, None], id_i[:, None], pos_j[None, :], id_j[None, :], inv_j[None, :])
    return out[:, 0]


def before(n):
    index = jnp.arange(n, dtype=jnp.int32)
    return (index[None, :] < index[:, None]).astype(BF)


def dot(a, b):
    return jnp.dot(a, b, preferred_element_type=jnp.float32)


def on_device(embeddings, assignment, prev_counts, old_centroids, block_owner):
    n_dp = lax.axis_size("dp")
    n_grp = lax.axis_size("group")
    grp = lax.axis_index("group")
    doc_rows, half = embeddings.shape
    cap = 2 * doc_rows // n_dp
    owned = old_centroids.shape[0]
    n_blocks = block_owner.shape[0]
    width = cap // CHUNKS
    mine = width // n_grp
    part_rows = n_dp * width

    owners = jnp.arange(n_dp, dtype=jnp.int32)
    owner_hot = (block_owner[:, None] == owners[None, :]).astype(BF)
    rank = jnp.sum(dot(before(n_blocks), owner_hot) * owner_hot.astype(jnp.float32), axis=1)
    table = jnp.concatenate([owner_hot, (rank + 1.0).astype(BF)[:, None]], axis=1)
    block_hot = (
        (assignment >> 6)[:, None] == jnp.arange(n_blocks, dtype=jnp.int32)[None, :]
    ).astype(BF)
    look = dot(block_hot, table)
    dest_hot = look[:, :n_dp]
    dest_bf = dest_hot.astype(BF)
    valid = assignment >= 0
    order_in = jnp.sum(dot(before(doc_rows), dest_bf) * dest_hot, axis=1).astype(jnp.int32)
    dest = jnp.sum(dest_hot * owners.astype(jnp.float32)[None, :], axis=1).astype(jnp.int32)
    slot = jnp.where(valid, dest * cap + order_in, -1)
    order_hot = order_in[:, None] == jnp.arange(cap, dtype=jnp.int32)[None, :]
    low = (assignment & (CB - 1)).astype(jnp.float32)
    fields = jnp.concatenate(
        [
            jnp.where(order_hot, look[:, n_dp :], 0.0).astype(BF),
            jnp.where(order_hot, low[:, None], 0.0).astype(BF),
        ],
        axis=1,
    )
    meta = lax.dot_general(
        dest_bf, fields, (((0,), (0,)), ((), ())), preferred_element_type=jnp.float32
    ).astype(jnp.int32)
    places = (meta[:, :cap] - 1) * CB + meta[:, cap:]

    got_places = lax.all_to_all(places, "dp", split_axis=0, concat_axis=0, tiled=True)

    got = []
    for c in range(CHUNKS):
        names = (owners[:, None] * cap + c * width + jnp.arange(width, dtype=jnp.int32)).reshape(-1)
        pick = (names[:, None] == slot[None, :]).astype(BF)
        outgoing = dot(pick, embeddings).astype(BF).reshape(n_dp, width, half)
        got.append(lax.all_to_all(outgoing, "dp", split_axis=0, concat_axis=0, tiled=True))

    flat = got_places.reshape(-1)
    taken = flat >= 0
    block_in = jnp.arange(owned // CB, dtype=jnp.int32)
    hot_a = ((flat >> 6)[None, :] == block_in[:, None]) & taken[None, :]
    hot_b = (flat & (CB - 1))[:, None] == jnp.arange(CB, dtype=jnp.int32)[None, :]
    counts = dot(hot_a.astype(BF), hot_b.astype(BF)).reshape(-1)
    prev = prev_counts.astype(jnp.float32)
    total = prev[:, None] * old_centroids

    ids = jnp.arange(part_rows, dtype=jnp.int32)

    def own_part(x):
        axis = x.ndim - 2 if x.ndim > 2 else 1
        return lax.dynamic_slice_in_dim(x, grp * mine, mine, axis)

    chunks = []
    for c in range(CHUNKS):
        place = got_places[:, c * width : (c + 1) * width]
        line = place.reshape(-1)
        hot = (jnp.arange(owned, dtype=jnp.int32)[:, None] == line[None, :]).astype(BF)
        total = total + dot(hot, got[c].reshape(part_rows, half))
        every = lax.all_gather(got[c], "group", axis=0)
        own = own_part(every).reshape(n_grp, n_dp * mine, half)
        every = every.reshape(n_grp, part_rows, half)
        squares = jnp.sum(jnp.square(every.astype(jnp.float32)), axis=(0, 2))
        inverse = lax.rsqrt(squares + 1e-06)
        own_place = own_part(place).reshape(-1)
        chunks.append(
            dict(
                every=every, own=own, inverse=inverse,
                place_j=jnp.where(line >= 0, line, -2),
                place_i=jnp.where(own_place >= 0, own_place, -1),
                id_i=own_part(ids.reshape(n_dp, width)).reshape(-1),
                own_inverse=own_part(inverse.reshape(n_dp, width)).reshape(-1),
            )
        )
    best = []
    for a, left in enumerate(chunks):
        top = None
        for b, right in enumerate(chunks):
            value = gram_best(
                a == b, left["own"], right["every"], left["place_i"], left["id_i"],
                right["place_j"], ids, right["inverse"],
            )
            top = value if top is None else jnp.maximum(top, value)
        best.append(jnp.maximum(top * left["own_inverse"], -1.0).reshape(n_dp, 1, mine))
    best = jnp.concatenate(best, axis=1).reshape(n_dp, 1, CHUNKS * mine)
    spread = jnp.broadcast_to(best, (n_dp, n_grp, CHUNKS * mine)).reshape(n_dp * n_grp, -1)
    returned = lax.all_to_all(spread, ("dp", "group"), split_axis=0, concat_axis=0, tiled=True)
    returned = returned.reshape(n_dp, n_grp, CHUNKS, mine).transpose(0, 2, 1, 3).reshape(n_dp, cap)
    rows = jnp.dot(
        dest_hot, returned, precision=lax.Precision.HIGHEST, preferred_element_type=jnp.float32
    )
    max_sim = jnp.sum(jnp.where(order_hot, rows, 0.0), axis=1)
    max_sim = jnp.where(valid, max_sim, -1.0)
    new_centroids = total / (prev + counts)[:, None]
    return (new_centroids, max_sim)


def solution(mesh):
    return jax.shard_map(
        on_device,
        mesh=mesh,
        in_specs=(P("dp", "group"), P("dp"), P("dp"), P("dp", "group"), P()),
        out_specs=(P("dp", "group"), P("dp")),
        check_vma=False,
    )
```

time: 405 us -> 235 us (0.58)
  local copies, waits for them, and re-layouts: 125 us -> 16.1 us
  waiting for transfers between devices: 124 us -> 82.3 us
  Pallas kernels: 0 us -> 29.8 us
  starting transfers between devices: 55.2 us -> 33.6 us
  other arithmetic: 25.5 us -> 10.4 us
  matrix products: 58.6 us -> 47.5 us
    gather x5 -> x0, local copies, waits for them, and re-layouts: 111 us -> none  [the longest x1 40.5 us: on_device(): send_ids = ids_pad[source_row].reshape(n_dp, cap)]
    all_to_all x1 -> x2, waiting for transfers between devices: 123 us -> 80.7 us  [on_device(): lax.all_to_all(outgoing, 'dp', split_axis=0, concat_axis=0, tiled=True)]
    pallas_call x0 -> x4, Pallas kernels: none -> 29.8 us  [gram_best(): pl.pallas_call(lambda *refs: gram_kernel(diagonal, *refs), grid=(rows //...]
    all_to_all x2, starting transfers between devices: 48 us -> 18.9 us  [the longest x1 9.97 us: on_device(): lax.all_to_all(places, 'dp', split_axis=0, concat_axis=0, tiled=True)]
    dot_general x2 -> x10, matrix products: 58.6 us -> 47.5 us  [the longest x8 44.9 us: dot(): return jnp.dot(a, b, preferred_element_type=jnp.float32)]
    reduce_sum x4 -> x3, other arithmetic: 15.2 us -> 4.21 us  [the longest x2 4.12 us: on_device(): squares = jnp.sum(jnp.square(every.astype(jnp.float32)), axis=(0, 2))]
    another operation x6 -> x0, other arithmetic: 9.44 us -> none
    scatter x1 -> x0, local copies, waits for them, and re-layouts: 8.07 us -> none  [on_device(): source_row = jnp.full((slots + 1,), doc_rows, jnp.int32).at[slot].set(jnp...]
  transfers between devices with their start and end apart: 4 -> 6, of which waited for: 1 -> 3; matrix products, arithmetic and copies ran while one was open for 38% -> 19% of each run, Pallas kernels for 0% -> 0%
where the time goes in v1:
time: 235 us; the launch traced here: 234 us
  waiting for transfers between devices  82.3 us (35%)
  matrix products  47.5 us (20%)
  starting transfers between devices  33.6 us (14%)
  Pallas kernels  29.8 us (13%)
  local copies, waits for them, and re-layouts  16.1 us (7%)
  between operations  14.4 us (6%)
  other arithmetic  10.4 us (4%)
    all_to_all x2, waiting for transfers between devices, on_device(): lax.all_to_all(outgoing, 'dp', split_axis=0, concat_axis=0, tiled=True)  80.7 us
    dot_general x8, matrix products, dot(): return jnp.dot(a, b, preferred_element_type=jnp.float32)  44.9 us
    pallas_call x4, Pallas kernels, gram_best(): pl.pallas_call(lambda *refs: gram_kernel(diagonal, *refs), grid=(rows //...  29.8 us
    all_to_all x2, starting transfers between devices, on_device(): lax.all_to_all(outgoing, 'dp', split_axis=0, concat_axis=0, tiled=True)  14.6 us
    all_to_all x1, starting transfers between devices, on_device(): lax.all_to_all(places, 'dp', split_axis=0, concat_axis=0, tiled=True)  9.97 us
    all_to_all x1, starting transfers between devices, on_device(): lax.all_to_all(spread, ('dp', 'group'), split_axis=0, concat_axis=0, tile...  8.9 us
    unnamed x23, local copies, waits for them, and re-layouts  6.63 us
    dynamic_slice x3, local copies, waits for them, and re-layouts, own_part(): return lax.dynamic_slice_in_dim(x, grp * mine, mine, axis)  4.9 us
  transfers between devices with their start and end apart: 6, of which 3 were waited for; matrix products, arithmetic and copies ran while one was open for 19% of the time, Pallas kernels for 0%

profile of v1, /device:TPU:0, one launch (start us, length us, event | category | flops | bytes accessed | tf_op | source)
XLA Modules:
  0.0 234.1 jit_solution(8915552958094097480)
XLA Ops:
  7.2 0.0 copy-start
  7.2 0.8 fusion.41
  8.0 1.3 fusion.31
  9.3 0.7 and_convert_fusion
  10.0 1.7 fusion.13
  11.7 1.5 fusion.29
  13.2 0.1 multiply_reduce_fusion.2
  13.3 0.1 add_bitcast_fusion.1
  13.4 5.7 %fusion.16 = bf16[2048,512]{1,0:T(8,128)(2,1)} fusion(bf16[2048,512]{1,0:T(8,128)(2,1)S(1)} %copy-done, s32[2048]{0:T(1024)S(1)} %get-tuple-element.2, s32[2048]{0:T(1024)S(1)} %add_bitcast_fusion.1), kind=kOutput, calls=%fused_computation.24 | convolution fusion | flops 4300210176 | bytes 4210688 | tf_op jit(solution)/shard_map/dot_general | solution.py:75
  19.1 8.4 %all-to-all-start.1 = ((bf16[16,128,512]{2,1,0:T(8,128)(2,1)}), bf16[16,128,512]{2,1,0:T(8,128)(2,1)}, u32[]{:S(2)}, u32[]{:S(2)}) async-start(bf16[16,128,512]{2,1,0:T(8,128)(2,1)} %bitcast.58), calls=%async_computation.1 | async-start | bytes 4194304 | tf_op jit(solution)/shard_map/all_to_all | solution.py:125
  27.5 0.4 select_convert_fusion.1
  28.0 0.6 fusion.32
  28.6 0.6 copy.37
  29.3 0.1 add_bitcast_fusion
  29.3 41.3 %all-to-all-done.1 = bf16[16,128,512]{2,1,0:T(8,128)(2,1)} async-done(((bf16[16,128,512]{2,1,0:T(8,128)(2,1)}), bf16[16,128,512]{2,1,0:T(8,128)(2,1)}, u32[]{:S(2)}, u32[]{:S(2)}) %all-to-all-start.1) | async-done | bytes 2097184 | tf_op jit(solution)/shard_map/all_to_all | solution.py:125
  70.6 10.0 %all-to-all-start = ((s32[16,1,256]{2,1,0:T(1,128)}), s32[16,1,256]{2,1,0:T(1,128)S(1)}, u32[]{:S(2)}, u32[]{:S(2)}) async-start(s32[16,1,256]{2,1,0:T(1,128)} %copy.37), calls=%async_computation | async-start | bytes 32768 | tf_op jit(solution)/shard_map/all_to_all | solution.py:118
  80.6 0.0 all-gather.5.cloned.1.call-start
  80.6 0.7 all-gather.5.cloned.1.call-update
  81.3 5.7 %fusion.19 = bf16[2048,512]{1,0:T(8,128)(2,1)} fusion(bf16[2048,512]{1,0:T(8,128)(2,1)S(1)} %copy-done, s32[2048]{0:T(1024)S(1)} %get-tuple-element.2, s32[2048]{0:T(1024)S(1)} %add_bitcast_fusion), kind=kOutput, calls=%fused_computation.25 | convolution fusion | flops 4300210176 | bytes 4210688 | tf_op jit(solution)/shard_map/dot_general | solution.py:75
  87.1 0.8 all-to-all-done
  87.9 6.2 %all-to-all-start.2 = ((bf16[16,128,512]{2,1,0:T(8,128)(2,1)}), bf16[16,128,512]{2,1,0:T(8,128)(2,1)}, u32[]{:S(2)}, u32[]{:S(2)}) async-start(bf16[16,128,512]{2,1,0:T(8,128)(2,1)} %bitcast.57), calls=%async_computation.2 | async-start | bytes 4194304 | tf_op jit(solution)/shard_map/all_to_all | solution.py:125
  94.2 0.0 all-gather.7.cloned.1.call-start
  94.2 0.5 broadcast_in_dim_reshape.3.refs_3_
  94.8 0.1 constant_dynamic-slice_fusion
  94.8 0.5 reshape.317
  95.3 1.3 reshape.318
  96.6 0.1 compare_reduce_fusion
  96.7 39.5 %all-to-all-done.2 = bf16[16,128,512]{2,1,0:T(8,128)(2,1)} async-done(((bf16[16,128,512]{2,1,0:T(8,128)(2,1)}), bf16[16,128,512]{2,1,0:T(8,128)(2,1)}, u32[]{:S(2)}, u32[]{:S(2)}) %all-to-all-start.2) | async-done | bytes 2097184 | tf_op jit(solution)/shard_map/all_to_all | solution.py:125
  136.2 0.0 all-gather.7.cloned.1.call-update
  136.2 0.8 fusion.27
  137.0 0.1 reshape.299
  137.1 0.9 compare_select_fusion.1.refs_2_
  137.9 1.1 compare_select_fusion.refs_2_
  139.1 12.9 %fusion = f32[4096,512]{1,0:T(8,128)} fusion(bf16[2048,512]{1,0:T(8,128)(2,1)} %bitcast.5, s32[2048]{0:T(1024)S(1)} %get-tuple-element.5), kind=kOutput, calls=%fused_computation.2 | convolution fusion | flops 8598323200 | bytes 10493952 | tf_op jit(solution)/shard_map/dot_general | solution.py:75
  151.9 3.3 %constant_dynamic-slice_fusion.3 = bf16[2,16,64,512]{3,2,1,0:T(8,128)(2,1)} fusion(bf16[2,16,128,512]{3,2,1,0:T(8,128)(2,1)} %bitcast.41, s32[]{:T(128)S(6)} %select_n.73), kind=kLoop, calls=%fused_computation.88 | loop fusion | bytes 4194308 | tf_op jit(solution)/shard_map/dynamic_slice | solution.py:140
  155.2 0.9 multiply_reduce_fusion.1
  156.1 0.0 all-gather.7.cloned.1.call-done
  156.2 3.2 %multiply_reduce_fusion = f32[16,128]{1,0:T(8,128)S(1)} fusion(bf16[2,16,128,512]{3,2,1,0:T(8,128)(2,1)} %bitcast.45), kind=kLoop, calls=%fused_computation.12 | loop fusion | flops 6289408 | bytes 4202496 | tf_op jit(solution)/shard_map/reduce_sum | solution.py:151
  159.4 0.2 copy-done.4
  159.6 1.5 constant_dynamic-slice_fusion.1
  161.2 1.6 copy-done.7
  162.8 1.0 copy-done.8
  163.8 7.7 %shard_map.68 = f32[1024,1]{1,0:T(8,128)S(1)} custom-call(bf16[2,1024,512]{2,1,0:T(8,128)(2,1)S(1)} %bitcast.51, bf16[2,2048,512]{2,1,0:T(8,128)(2,1)S(1)} %bitcast.43, s32[1024,1]{1,0:T(8,128)S(1)} %copy-done.8, s32[1024,1]{1,0:T(8,128)S(1)} %broadcast_in_dim_reshape.3.refs_3_, s32[1,2048]{1,0:T(1,128)S(1)} %compare_select_fusion.3.refs_4_, ...), custom_call_target="tpu_custom_call" | custom-call | flops 4294967296 | bytes 10485760 | tf_op jit(solution)/shard_map/pallas_call | solution.py:48
  171.5 7.2 %shard_map.69 = f32[1024,1]{1,0:T(8,128)S(1)} custom-call(bf16[2,1024,512]{2,1,0:T(8,128)(2,1)S(1)} %bitcast.52, bf16[2,2048,512]{2,1,0:T(8,128)(2,1)S(1)} %bitcast.47, s32[1024,1]{1,0:T(8,128)S(1)} %copy-done.8, s32[1024,1]{1,0:T(8,128)S(1)} %broadcast_in_dim_reshape.3.refs_3_, s32[1,2048]{1,0:T(1,128)S(1)} %compare_select_fusion.2.refs_4_, ...), custom_call_target="tpu_custom_call" | custom-call | flops 4294967296 | bytes 10485760 | tf_op jit(solution)/shard_map/pallas_call | solution.py:48
  178.7 0.2 maximum_reduce_fusion.1
  178.9 0.1 max.31
  179.0 0.1 maximum_bitcast_fusion.1
  179.1 2.2 copy-done.3
  181.3 1.6 copy-done.6
  182.9 7.2 %shard_map.70 = f32[1024,1]{1,0:T(8,128)S(1)} custom-call(bf16[2,1024,512]{2,1,0:T(8,128)(2,1)S(1)} %bitcast.49, bf16[2,2048,512]{2,1,0:T(8,128)(2,1)S(1)} %bitcast.44, s32[1024,1]{1,0:T(8,128)S(1)} %compare_select_fusion.refs_2_, s32[1024,1]{1,0:T(8,128)S(1)} %broadcast_in_dim_reshape.3.refs_3_, s32[1,2048]{1,0:T(1,128)S(1)} %compare_select_fusion.3.refs_4_, ...), custom_call_target="tpu_custom_call" | custom-call | flops 4294967296 | bytes 10485760 | tf_op jit(solution)/shard_map/pallas_call | solution.py:48
  190.1 7.7 %shard_map.71 = f32[1024,1]{1,0:T(8,128)S(1)} custom-call(bf16[2,1024,512]{2,1,0:T(8,128)(2,1)S(1)} %bitcast.50, bf16[2,2048,512]{2,1,0:T(8,128)(2,1)S(1)} %bitcast.48, s32[1024,1]{1,0:T(8,128)S(1)} %compare_select_fusion.refs_2_, s32[1024,1]{1,0:T(8,128)S(1)} %broadcast_in_dim_reshape.3.refs_3_, s32[1,2048]{1,0:T(1,128)S(1)} %compare_select_fusion.2.refs_4_, ...), custom_call_target="tpu_custom_call" | custom-call | flops 4294967296 | bytes 10485760 | tf_op jit(solution)/shard_map/pallas_call | solution.py:48
  197.8 0.2 maximum_reduce_fusion
  198.0 0.1 max.35
  198.1 0.1 maximum_bitcast_fusion
  198.2 0.1 broadcast_in_dim.48
  198.3 0.6 broadcast_in_dim.49
  198.9 8.9 %all-to-all-start.3 = ((f32[32,1,128]{2,1,0:T(1,128)}), f32[32,1,128]{2,1,0:T(1,128)S(1)}, u32[]{:S(2)}, u32[]{:S(2)}) async-start(f32[32,1,128]{2,1,0:T(1,128)} %bitcast.24), calls=%async_computation.3 | async-start | bytes 32768 | tf_op jit(solution)/shard_map/all_to_all | solution.py:175
  207.8 15.4 %add_divide_fusion = f32[4096,512]{1,0:T(8,128)} fusion(f32[4096,512]{1,0:T(8,128)} %fusion, f32[4096,512]{1,0:T(8,128)} %param.8, bf16[2048,512]{1,0:T(8,128)(2,1)} %bitcast.9, s32[2048]{0:T(1024)S(1)} %get-tuple-element.6, f32[4096]{0:T(1024)S(1)} %convert_add_fusion, f32[4096]{0:T(1024)S(1)} %convert_element_type.77), kind=kOutput, calls=%fused_computation.14 | convolution fusion | flops 8606711808 | bytes 27303936 | tf_op jit(solution)/shard_map/dot_general | solution.py:75
  223.2 0.5 broadcast.188
  223.7 0.7 reduce.11
  224.4 0.1 reshape.311
  224.5 0.1 reshape.312
  224.6 2.0 fusion.28
  226.6 0.6 broadcast_select_fusion
  (45 shorter events, 0.3 us)
Async XLA Ops:
  7.2 6.2 %copy-start = (bf16[2048,512]{1,0:T(8,128)(2,1)S(1)}, bf16[2048,512]{1,0:T(8,128)(2,1)}, u32[]{:S(2)}) copy-start(bf16[2048,512]{1,0:T(8,128)(2,1)} %param.5) | copy-start | bytes 6291460
  10.0 3.3 %copy-start.10 = (s32[2048]{0:T(1024)S(1)}, s32[2048]{0:T(1024)}, u32[]{:S(2)}) copy-start(s32[2048]{0:T(1024)} %param.6) | copy-start | bytes 24580
  19.1 51.5 %all-to-all-start.1 = ((bf16[16,128,512]{2,1,0:T(8,128)(2,1)}), bf16[16,128,512]{2,1,0:T(8,128)(2,1)}, u32[]{:S(2)}, u32[]{:S(2)}) async-start(bf16[16,128,512]{2,1,0:T(8,128)(2,1)} %bitcast.58), calls=%async_computation.1 | async-start | bytes 4194304 | tf_op jit(solution)/shard_map/all_to_all | solution.py:125
  70.6 17.3 %all-to-all-start = ((s32[16,1,256]{2,1,0:T(1,128)}), s32[16,1,256]{2,1,0:T(1,128)S(1)}, u32[]{:S(2)}, u32[]{:S(2)}) async-start(s32[16,1,256]{2,1,0:T(1,128)} %copy.37), calls=%async_computation | async-start | bytes 32768 | tf_op jit(solution)/shard_map/all_to_all | solution.py:118
  80.6 71.3 %all-gather.5.cloned.1.call-start = ((), (), s32[]{:S(2)}) async-start(), calls=%async_computation.4 | async-start | bytes 6291456 | tf_op jit(solution)/shard_map/all_gather | solution.py:148
  87.1 7.6 %copy-start.9 = (s32[4096]{0:T(1024)S(1)}, s32[4096]{0:T(1024)}, u32[]{:S(2)}) copy-start(s32[4096]{0:T(1024)} %param.7) | copy-start | bytes 49156
  87.9 48.2 %all-to-all-start.2 = ((bf16[16,128,512]{2,1,0:T(8,128)(2,1)}), bf16[16,128,512]{2,1,0:T(8,128)(2,1)}, u32[]{:S(2)}, u32[]{:S(2)}) async-start(bf16[16,128,512]{2,1,0:T(8,128)(2,1)} %bitcast.57), calls=%async_computation.2 | async-start | bytes 4194304 | tf_op jit(solution)/shard_map/all_to_all | solution.py:125
  94.2 62.0 %all-gather.7.cloned.1.call-start = ((), (), s32[]{:S(2)}) async-start(), calls=%async_computation.5 | async-start | bytes 6291456 | tf_op jit(solution)/shard_map/all_gather | solution.py:148
  151.9 3.3 %copy-start.1 = (bf16[32,128,512]{2,1,0:T(8,128)(2,1)S(1)}, bf16[32,128,512]{2,1,0:T(8,128)(2,1)}, u32[]{:S(2)}) copy-start(bf16[32,128,512]{2,1,0:T(8,128)(2,1)} %all-gather.5.cloned.1.call-done) | copy-start | bytes 12582916
  156.2 3.5 %copy-start.4 = (bf16[32,128,512]{2,1,0:T(8,128)(2,1)S(1)}, bf16[32,128,512]{2,1,0:T(8,128)(2,1)}, u32[]{:S(2)}) copy-start(bf16[32,128,512]{2,1,0:T(8,128)(2,1)} %all-gather.7.cloned.1.call-done) | copy-start | bytes 12582916
  156.2 5.0 %copy-start.2 = (bf16[32,128,512]{2,1,0:T(8,128)(2,1)S(1)}, bf16[32,128,512]{2,1,0:T(8,128)(2,1)}, u32[]{:S(2)}) copy-start(bf16[32,128,512]{2,1,0:T(8,128)(2,1)} %all-gather.5.cloned.1.call-done) | copy-start | bytes 12582916
  161.2 1.6 copy-start.7
  162.8 1.0 copy-start.8
  179.1 2.2 copy-start.3
  181.3 1.6 copy-start.6
  182.9 7.2 %copy-start.5 = (bf16[32,128,512]{2,1,0:T(8,128)(2,1)S(1)}, bf16[32,128,512]{2,1,0:T(8,128)(2,1)}, u32[]{:S(2)}) copy-start(bf16[32,128,512]{2,1,0:T(8,128)(2,1)} %all-gather.7.cloned.1.call-done) | copy-start | bytes 12582916
  198.9 24.3 %all-to-all-start.3 = ((f32[32,1,128]{2,1,0:T(1,128)}), f32[32,1,128]{2,1,0:T(1,128)S(1)}, u32[]{:S(2)}, u32[]{:S(2)}) async-start(f32[32,1,128]{2,1,0:T(1,128)} %bitcast.24), calls=%async_computation.3 | async-start | bytes 32768 | tf_op jit(solution)/shard_map/all_to_all | solution.py:175
Sparse Core Ops, SparseCore 0:
  83.0 14.9 all-gather.4
  136.3 17.7 all-gather.6

commit v2 on v1

v2 whole, which is shorter than its diff:
```python
import jax
import jax.numpy as jnp
from jax import lax
from jax.experimental import pallas as pl
from jax.experimental.pallas import tpu as pltpu
from jax.sharding import PartitionSpec as P

CB = 64
EXTRA = 16
NEG = -3.0e38
BF = jnp.bfloat16


def gram_kernel(diagonal, own_ref, all_ref, key_i, key_j, inv_j, out_ref, best):
    j = pl.program_id(1)

    @pl.when(j == 0)
    def _():
        best[...] = jnp.full_like(best, NEG)

    gram = None
    for part in range(own_ref.shape[0]):
        term = lax.dot_general(
            own_ref[part], all_ref[part], (((1,), (1,)), ((), ())),
            preferred_element_type=jnp.float32,
        )
        gram = term if gram is None else gram + term
    same = key_i[:, 0:1] == key_j[0:1, :]
    if diagonal:
        same = same & (key_i[:, 1:2] != key_j[1:2, :])
    value = jnp.where(same, gram * inv_j[...], NEG)
    top = best[...]
    for lane in range(0, value.shape[1], 128):
        top = jnp.maximum(top, value[:, lane : lane + 128])
    best[...] = top

    @pl.when(j == pl.num_programs(1) - 1)
    def _():
        out_ref[...] = jnp.max(best[...], axis=1, keepdims=True)


def tile(size, step, most):
    return max([n for n in range(step, most + 1, step) if size % n == 0], default=size)


def gram_best(diagonal, own, every, key_i, key_j, inv_j):
    parts, rows, half = own.shape
    cols = every.shape[1]
    ti, tj = tile(rows, 16, 640), tile(cols, 128, 512)
    out = pl.pallas_call(
        lambda *refs: gram_kernel(diagonal, *refs),
        grid=(rows // ti, cols // tj),
        in_specs=[
            pl.BlockSpec((parts, ti, half), lambda i, j: (0, i, 0)),
            pl.BlockSpec((parts, tj, half), lambda i, j: (0, j, 0)),
            pl.BlockSpec((ti, 2), lambda i, j: (i, 0)),
            pl.BlockSpec((2, tj), lambda i, j: (0, j)),
            pl.BlockSpec((1, tj), lambda i, j: (0, j)),
        ],
        out_specs=pl.BlockSpec((ti, 1), lambda i, j: (i, 0)),
        out_shape=jax.ShapeDtypeStruct((rows, 1), jnp.float32),
        scratch_shapes=[pltpu.VMEM((ti, 128), jnp.float32)],
        compiler_params=pltpu.CompilerParams(vmem_limit_bytes=40 * 1024 * 1024),
        cost_estimate=pl.CostEstimate(
            flops=2 * rows * cols * parts * half,
            bytes_accessed=2 * parts * half * (rows + cols * (rows // ti)),
            transcendentals=0,
        ),
    )(own, every, key_i, key_j, inv_j[None, :])
    return out[:, 0]


def before(n):
    index = jnp.arange(n, dtype=jnp.int32)
    return (index[None, :] < index[:, None]).astype(BF)


def dot(a, b):
    return jnp.dot(a, b, preferred_element_type=jnp.float32)


def on_device(embeddings, assignment, prev_counts, old_centroids, block_owner):
    n_dp = lax.axis_size("dp")
    n_grp = lax.axis_size("group")
    grp = lax.axis_index("group")
    doc_rows, half = embeddings.shape
    cap = 2 * doc_rows // n_dp
    owned = old_centroids.shape[0]
    n_blocks = block_owner.shape[0]
    first = cap * 5 // 8
    starts, widths = (0, first), (first, cap - first)
    heights = (first + EXTRA, cap - first)

    owners = jnp.arange(n_dp, dtype=jnp.int32)
    owner_hot = (block_owner[:, None] == owners[None, :]).astype(BF)
    rank = jnp.sum(dot(before(n_blocks), owner_hot) * owner_hot.astype(jnp.float32), axis=1)
    table = jnp.concatenate([owner_hot, (rank + 1.0).astype(BF)[:, None]], axis=1)
    block_hot = (
        (assignment >> 6)[:, None] == jnp.arange(n_blocks, dtype=jnp.int32)[None, :]
    ).astype(BF)
    look = dot(block_hot, table)
    dest_hot = look[:, :n_dp]
    dest_bf = dest_hot.astype(BF)
    valid = assignment >= 0
    order_in = jnp.sum(dot(before(doc_rows), dest_bf) * dest_hot, axis=1).astype(jnp.int32)
    dest = jnp.sum(dest_hot * owners.astype(jnp.float32)[None, :], axis=1).astype(jnp.int32)
    slot = jnp.where(valid, dest * cap + order_in, -1)
    order_hot = order_in[:, None] == jnp.arange(cap, dtype=jnp.int32)[None, :]
    low = (assignment & (CB - 1)).astype(jnp.float32)
    fields = jnp.concatenate(
        [
            jnp.where(order_hot, look[:, n_dp :], 0.0).astype(BF),
            jnp.where(order_hot, low[:, None], 0.0).astype(BF),
        ],
        axis=1,
    )
    meta = lax.dot_general(
        dest_bf, fields, (((0,), (0,)), ((), ())), preferred_element_type=jnp.float32
    )
    meta = jnp.pad(meta, ((0, 0), (0, EXTRA * half - 2 * cap))).reshape(n_dp, EXTRA, half)
    meta = jnp.pad(meta, ((0, 0), (first, 0), (0, 0)))

    outgoing = []
    for c in range(2):
        row = jnp.arange(heights[c], dtype=jnp.int32)
        names = jnp.where(row < widths[c], owners[:, None] * cap + starts[c] + row, -2).reshape(-1)
        pick = (names[:, None] == slot[None, :]).astype(BF)
        rows = dot(pick, embeddings).reshape(n_dp, heights[c], half)
        outgoing.append((rows if c else rows + meta).astype(BF))
    early = lax.all_to_all(outgoing[0], "dp", split_axis=0, concat_axis=0, tiled=True)
    early, later = lax.optimization_barrier((early, outgoing[1]))
    got = [early, lax.all_to_all(later, "dp", split_axis=0, concat_axis=0, tiled=True)]
    fields = got[0][:, first:].reshape(n_dp, -1).astype(jnp.float32).astype(jnp.int32)
    got_places = (fields[:, :cap] - 1) * CB + fields[:, cap : 2 * cap]

    flat = got_places.reshape(-1)
    taken = flat >= 0
    block_in = jnp.arange(owned // CB, dtype=jnp.int32)
    hot_a = ((flat >> 6)[None, :] == block_in[:, None]) & taken[None, :]
    hot_b = (flat & (CB - 1))[:, None] == jnp.arange(CB, dtype=jnp.int32)[None, :]
    counts = dot(hot_a.astype(BF), hot_b.astype(BF)).reshape(-1)
    prev = prev_counts.astype(jnp.float32)
    total = prev[:, None] * old_centroids

    def gram_pair(left, right):
        return gram_best(
            left is right, left["own"], right["every"], left["key_i"], right["key_j"],
            right["inverse"],
        )

    chunks = []
    for c in range(2):
        if c:
            total, corner, got[c] = lax.optimization_barrier((total, corner, got[c]))
        mine, height = widths[c] // n_grp, heights[c]
        part_rows = n_dp * height

        def own_part(x, axis):
            return lax.dynamic_slice_in_dim(x, grp * mine, mine, axis)

        place = got_places[:, starts[c] : starts[c] + widths[c]]
        place = jnp.pad(place, ((0, 0), (0, height - widths[c])), constant_values=-1)
        line = place.reshape(-1)
        hot = (jnp.arange(owned, dtype=jnp.int32)[:, None] == line[None, :]).astype(BF)
        total = total + dot(hot, got[c].reshape(part_rows, half))
        every = lax.all_gather(got[c], "group", axis=0)
        own = own_part(every, 2).reshape(n_grp, n_dp * mine, half)
        every = every.reshape(n_grp, part_rows, half)
        squares = jnp.sum(jnp.square(every.astype(jnp.float32)), axis=(0, 2))
        inverse = lax.rsqrt(squares + 1e-06)
        ids = jnp.arange(part_rows, dtype=jnp.int32)
        own_place = own_part(place, 1).reshape(-1)
        own_ids = own_part(ids.reshape(n_dp, height), 1).reshape(-1)
        chunks.append(
            dict(
                every=every, own=own, inverse=inverse,
                key_i=jnp.stack([jnp.where(own_place >= 0, own_place, -1), own_ids], axis=1),
                key_j=jnp.stack([jnp.where(line >= 0, line, -2), ids], axis=0),
                own_inverse=own_part(inverse.reshape(n_dp, height), 1).reshape(-1),
            )
        )
        if c == 0:
            corner = gram_pair(chunks[0], chunks[0])
    one, two = chunks
    tops = (
        jnp.maximum(corner, gram_pair(one, two)),
        jnp.maximum(gram_pair(two, one), gram_pair(two, two)),
    )
    best = [
        jnp.maximum(top * x["own_inverse"], -1.0).reshape(n_dp, -1) for top, x in zip(tops, chunks)
    ]
    best = jnp.concatenate(best, axis=1)
    spread = jnp.broadcast_to(best[:, None], (n_dp, n_grp, cap // n_grp)).reshape(n_dp * n_grp, -1)
    returned = lax.all_to_all(spread, ("dp", "group"), split_axis=0, concat_axis=0, tiled=True)
    returned = returned.reshape(n_dp, n_grp, cap // n_grp)
    cut = first // n_grp
    returned = jnp.concatenate(
        [returned[:, :, :cut].reshape(n_dp, -1), returned[:, :, cut:].reshape(n_dp, -1)], axis=1
    )
    rows = jnp.dot(
        dest_hot, returned, precision=lax.Precision.HIGHEST, preferred_element_type=jnp.float32
    )
    max_sim = jnp.sum(jnp.where(order_hot, rows, 0.0), axis=1)
    max_sim = jnp.where(valid, max_sim, -1.0)
    new_centroids = total / (prev + counts)[:, None]
    return (new_centroids, max_sim)


def solution(mesh):
    return jax.shard_map(
        on_device,
        mesh=mesh,
        in_specs=(P("dp", "group"), P("dp"), P("dp"), P("dp", "group"), P()),
        out_specs=(P("dp", "group"), P("dp")),
        check_vma=False,
    )
```

time: 235 us -> 224 us (0.953)
  waiting for transfers between devices: 82.3 us -> 60.6 us
  Pallas kernels: 29.8 us -> 35.9 us
  other arithmetic: 10.4 us -> 16.3 us
  starting transfers between devices: 33.6 us -> 28.4 us
  local copies, waits for them, and re-layouts: 16.1 us -> 19.1 us
    all_to_all x3 -> x2, waiting for transfers between devices: 81.6 us -> 51.3 us  [the longest x1 51.3 us: on_device(): lax.all_to_all(outgoing[0], 'dp', split_axis=0, concat_axis=0, tiled=True)]
    all_gather x2, waiting for transfers between devices: 0.02 us -> 9.19 us  [on_device(): every = lax.all_gather(got[c], 'group', axis=0)]
    pallas_call x4, Pallas kernels: 29.8 us -> 35.9 us  [gram_best(): pl.pallas_call(lambda *refs: gram_kernel(diagonal, *refs), grid=(rows //...]
    unnamed x23 -> x42, local copies, waits for them, and re-layouts: 6.63 us -> 11.2 us
    all_to_all x1, starting transfers between devices: 8.9 us -> 5.99 us  [on_device(): lax.all_to_all(spread, ('dp', 'group'), split_axis=0, concat_axis=0, tile...]
    reduce_sum x2, other arithmetic: 4.12 us -> 6.61 us  [on_device(): squares = jnp.sum(jnp.square(every.astype(jnp.float32)), axis=(0, 2))]
    all_to_all x3 -> x2, starting transfers between devices: 24.6 us -> 22.1 us  [the longest x1 13.8 us: on_device(): lax.all_to_all(later, 'dp', split_axis=0, concat_axis=0, tiled=True)]
    convert_element_type x1 -> x2, other arithmetic: 0.7 us -> 3.11 us  [the longest x1 2.08 us: on_device(): outgoing.append((rows if c else rows + meta).astype(BF))]
  transfers between devices with their start and end apart: 6 -> 5, of which waited for: 3 -> 2; matrix products, arithmetic and copies ran while one was open for 19% -> 21% of each run, Pallas kernels for 0% -> 6%
where the time goes in v2:
time: 224 us
  waiting for transfers between devices  60.6 us (27%)
  matrix products  48.8 us (22%)
  Pallas kernels  35.9 us (16%)
  starting transfers between devices  28.4 us (13%)
  local copies, waits for them, and re-layouts  19.1 us (9%)
  other arithmetic  16.3 us (7%)
  between operations  14.6 us (7%)
    all_to_all x1, waiting for transfers between devices, on_device(): lax.all_to_all(outgoing[0], 'dp', split_axis=0, concat_axis=0, tiled=True)  51.3 us
    dot_general x8, matrix products, dot(): return jnp.dot(a, b, preferred_element_type=jnp.float32)  46.1 us
    pallas_call x4, Pallas kernels, gram_best(): pl.pallas_call(lambda *refs: gram_kernel(diagonal, *refs), grid=(rows //...  35.9 us
    all_to_all x1, starting transfers between devices, on_device(): lax.all_to_all(later, 'dp', split_axis=0, concat_axis=0, tiled=True)  13.8 us
    unnamed x42, local copies, waits for them, and re-layouts  11.2 us
    all_gather x2, waiting for transfers between devices, on_device(): every = lax.all_gather(got[c], 'group', axis=0)  9.19 us
    all_to_all x1, starting transfers between devices, on_device(): lax.all_to_all(outgoing[0], 'dp', split_axis=0, concat_axis=0, tiled=True)  8.36 us
    reduce_sum x2, other arithmetic, on_device(): squares = jnp.sum(jnp.square(every.astype(jnp.float32)), axis=(0, 2))  6.61 us
  transfers between devices with their start and end apart: 5, of which 2 were waited for; matrix products, arithmetic and copies ran while one was open for 21% of the time, Pallas kernels for 6%

profile of v2, /device:TPU:0, one launch (start us, length us, event | category | flops | bytes accessed | tf_op | source)
XLA Modules:
  0.0 223.7 jit_solution(18087190704182885348)
XLA Ops:
  7.2 0.8 fusion.35
  8.0 1.3 fusion.28
  9.3 0.7 broadcast_shift-right-arithmetic_fusion
  10.0 1.7 fusion.11
  11.7 1.5 fusion.26
  13.2 0.1 multiply_reduce_fusion.2
  13.4 0.4 select_convert_fusion.1
  13.8 0.6 fusion.20
  14.5 0.3 copy.17
  14.9 0.1 select_n.98
  15.0 6.4 %fusion.3 = f32[2816,512]{1,0:T(8,128)S(1)} fusion(bf16[2048,512]{1,0:T(8,128)(2,1)S(1)} %copy-done, s32[2048]{0:T(1024)S(1)} %get-tuple-element.14, s32[2816]{0:T(1024)S(1)} %select_n.98), kind=kOutput, calls=%fused_computation.5 | convolution fusion | flops 5911347200 | bytes 7883776 | tf_op jit(solution)/shard_map/dot_general | solution.py:79
  21.4 2.1 add_convert_fusion
  23.5 8.4 %all-to-all-start = ((bf16[16,176,512]{2,1,0:T(8,128)(2,1)}), bf16[16,176,512]{2,1,0:T(8,128)(2,1)}, u32[]{:S(2)}, u32[]{:S(2)}) async-start(bf16[16,176,512]{2,1,0:T(8,128)(2,1)} %add_convert_fusion), calls=%async_computation | async-start | bytes 5767168 | tf_op jit(solution)/shard_map/all_to_all | solution.py:130
  31.8 0.2 all-gather.5.cloned.1.call-start
  32.3 4.8 %fusion.16 = bf16[1536,512]{1,0:T(8,128)(2,1)} fusion(bf16[2048,512]{1,0:T(8,128)(2,1)S(1)} %copy-done, s32[2048]{0:T(1024)S(1)} %get-tuple-element.14, s32[1536]{0:T(1024)S(1)} %select_n.103), kind=kOutput, calls=%fused_computation.26 | convolution fusion | flops 3225157632 | bytes 3684352 | tf_op jit(solution)/shard_map/dot_general | solution.py:79
  37.0 51.3 %all-to-all-done = bf16[16,176,512]{2,1,0:T(8,128)(2,1)} async-done(((bf16[16,176,512]{2,1,0:T(8,128)(2,1)}), bf16[16,176,512]{2,1,0:T(8,128)(2,1)}, u32[]{:S(2)}, u32[]{:S(2)}) %all-to-all-start) | async-done | bytes 2883616 | tf_op jit(solution)/shard_map/all_to_all | solution.py:130
  88.4 1.0 convert_convert_fusion
  89.4 0.3 copy.18
  89.8 0.1 eq.137
  89.9 0.1 add_add_fusion.1
  89.9 0.1 reshape.315
  90.0 13.8 %all-to-all-start.1 = ((bf16[16,96,512]{2,1,0:T(8,128)(2,1)}), bf16[16,96,512]{2,1,0:T(8,128)(2,1)}, u32[]{:S(2)}, u32[]{:S(2)}) async-start(bf16[16,96,512]{2,1,0:T(8,128)(2,1)} %bitcast.44), calls=%async_computation.1 | async-start | bytes 3145728 | tf_op jit(solution)/shard_map/all_to_all | solution.py:132
  103.8 18.2 %multiply_add_fusion = f32[4096,512]{1,0:T(8,128)} fusion(f32[4096,512]{1,0:T(8,128)} %param.8, bf16[2816,512]{1,0:T(8,128)(2,1)} %bitcast.3, s32[2816]{0:T(1024)S(1)} %eq.137, f32[4096]{0:T(1024)S(1)} %convert_element_type.91), kind=kOutput, calls=%fused_computation.17 | convolution fusion | flops 11826888704 | bytes 19688448 | tf_op jit(solution)/shard_map/dot_general | solution.py:79
  122.0 0.1 reshape.319
  122.1 0.1 stack_reshape.6
  122.2 0.3 copy.13.refs_2_
  122.6 3.9 %multiply_reduce_fusion = f32[16,176]{1,0:T(8,128)S(1)} fusion(bf16[2,16,176,512]{3,2,1,0:T(8,128)(2,1)} %bitcast.28), kind=kLoop, calls=%fused_computation.12 | loop fusion | flops 8647936 | bytes 5778432 | tf_op jit(solution)/shard_map/reduce_sum | solution.py:169
  126.5 0.1 rsqrt.29.refs_4_
  126.6 1.9 constant_dynamic-slice_fusion.4
  128.6 2.6 %copy-done.1 = bf16[32,176,512]{2,1,0:T(8,128)(2,1)S(1)} copy-done((bf16[32,176,512]{2,1,0:T(8,128)(2,1)S(1)}, bf16[32,176,512]{2,1,0:T(8,128)(2,1)}, u32[]{:S(2)}) %copy-start.1) | copy-done | bytes 5767192
  131.2 13.9 %shard_map.68 = f32[1280,1]{1,0:T(8,128)S(1)} custom-call(bf16[2,1280,512]{2,1,0:T(8,128)(2,1)S(1)} %bitcast.36, bf16[2,2816,512]{2,1,0:T(8,128)(2,1)S(1)} %bitcast.30, s32[1280,2]{1,0:T(8,128)S(1)} %copy.13.refs_2_, s32[2,2816]{1,0:T(2,128)S(1)} %pad_add_fusion.refs_3_, f32[1,2816]{1,0:T(1,128)S(1)} %rsqrt.29.refs_4_), custom_call_target="tpu_custom_call" | custom-call | flops 7381975040 | bytes 14155776 | tf_op jit(solution)/shard_map/pallas_call | solution.py:50
  145.1 1.5 copy-done.5
  146.6 0.8 reduce.2
  147.5 0.1 reshape.323
  147.6 0.7 eq.141
  148.3 0.1 reshape.327
  148.4 0.1 stack_reshape.7
  148.5 1.0 copy.15.refs_2_
  149.6 0.8 fusion.24
  150.4 0.6 convert_add_fusion
  151.1 0.7 reshape.324
  151.8 9.2 %all-gather.7.cloned.1.call-done = bf16[32,96,512]{2,1,0:T(8,128)(2,1)} async-done(((bf16[16,96,512]{2,1,0:T(8,128)(2,1)}), bf16[32,96,512]{2,1,0:T(8,128)(2,1)}) %all-gather.7.cloned.1.call-update) | async-done | bytes 3145744 | tf_op jit(solution)/shard_map/all_gather | solution.py:166
  161.0 2.7 %multiply_reduce_fusion.1 = f32[16,96]{1,0:T(8,128)S(1)} fusion(bf16[2,16,96,512]{3,2,1,0:T(8,128)(2,1)} %bitcast.32), kind=kLoop, calls=%fused_computation.19 | loop fusion | flops 4717056 | bytes 3151872 | tf_op jit(solution)/shard_map/reduce_sum | solution.py:169
  163.7 0.1 copy-done.3
  163.8 1.3 constant_dynamic-slice_fusion.1
  165.1 0.1 rsqrt.31.refs_4_
  165.2 1.9 copy-done.4
  167.1 1.7 copy-done.6
  168.8 6.4 %shard_map.69 = f32[1280,1]{1,0:T(8,128)S(1)} custom-call(bf16[2,1280,512]{2,1,0:T(8,128)(2,1)S(1)} %bitcast.37, bf16[2,1536,512]{2,1,0:T(8,128)(2,1)S(1)} %bitcast.34, s32[1280,2]{1,0:T(8,128)S(1)} %copy.13.refs_2_, s32[2,1536]{1,0:T(2,128)S(1)} %pad_add_fusion.1.refs_3_, f32[1,1536]{1,0:T(1,128)S(1)} %rsqrt.31.refs_4_), custom_call_target="tpu_custom_call" | custom-call | flops 4026531840 | bytes 8912896 | tf_op jit(solution)/shard_map/pallas_call | solution.py:50
  175.2 4.9 %shard_map.71 = f32[768,1]{1,0:T(8,128)S(1)} custom-call(bf16[2,768,512]{2,1,0:T(8,128)(2,1)S(1)} %bitcast.38, bf16[2,1536,512]{2,1,0:T(8,128)(2,1)S(1)} %bitcast.35, s32[768,2]{1,0:T(8,128)S(1)} %copy-done.8, s32[2,1536]{1,0:T(2,128)S(1)} %pad_add_fusion.1.refs_3_, f32[1,1536]{1,0:T(1,128)S(1)} %rsqrt.31.refs_4_), custom_call_target="tpu_custom_call" | custom-call | flops 2415919104 | bytes 7864320 | tf_op jit(solution)/shard_map/pallas_call | solution.py:50
  180.2 2.6 %copy-done.2 = bf16[32,176,512]{2,1,0:T(8,128)(2,1)S(1)} copy-done((bf16[32,176,512]{2,1,0:T(8,128)(2,1)S(1)}, bf16[32,176,512]{2,1,0:T(8,128)(2,1)}, u32[]{:S(2)}) %copy-start.2) | copy-done | bytes 5767192
  182.8 10.8 %shard_map.70 = f32[768,1]{1,0:T(8,128)S(1)} custom-call(bf16[2,768,512]{2,1,0:T(8,128)(2,1)S(1)} %bitcast.39, bf16[2,2816,512]{2,1,0:T(8,128)(2,1)S(1)} %bitcast.31, s32[768,2]{1,0:T(8,128)S(1)} %copy-done.8, s32[2,2816]{1,0:T(2,128)S(1)} %copy-done.10, f32[1,2816]{1,0:T(1,128)S(1)} %rsqrt.29.refs_4_), custom_call_target="tpu_custom_call" | custom-call | flops 4429185024 | bytes 13107200 | tf_op jit(solution)/shard_map/pallas_call | solution.py:50
  193.6 0.2 reduce.3
  193.8 0.7 multiply_maximum_fusion.1
  194.6 0.2 maximum_reduce_fusion
  194.9 0.8 multiply_maximum_fusion
  195.7 0.1 pad_maximum_fusion
  195.7 0.6 broadcast_in_dim.113
  196.3 6.0 %all-to-all-start.2 = ((f32[32,1,128]{2,1,0:T(1,128)}), f32[32,1,128]{2,1,0:T(1,128)S(1)}, u32[]{:S(2)}, u32[]{:S(2)}) async-start(f32[32,1,128]{2,1,0:T(1,128)} %bitcast.11), calls=%async_computation.2 | async-start | bytes 32768 | tf_op jit(solution)/shard_map/all_to_all | solution.py:194
  202.4 11.6 %add_divide_fusion = f32[4096,512]{1,0:T(8,128)} fusion(f32[4096,512]{1,0:T(8,128)} %multiply_add_fusion, bf16[1536,512]{1,0:T(8,128)(2,1)} %bitcast.7, s32[1536]{0:T(1024)} %eq.141, f32[4096]{0:T(1024)} %convert_add_fusion), kind=kOutput, calls=%fused_computation.15 | convolution fusion | flops 6452936704 | bytes 18372608 | tf_op jit(solution)/shard_map/dot_general | solution.py:79
  214.1 0.1 reshape.333
  214.2 0.1 reshape.332
  214.2 2.0 fusion.25
  216.3 0.6 broadcast_select_fusion
  (78 shorter events, 1.2 us)
Async XLA Ops:
  7.2 7.8 %copy-start = (bf16[2048,512]{1,0:T(8,128)(2,1)S(1)}, bf16[2048,512]{1,0:T(8,128)(2,1)}, u32[]{:S(2)}) copy-start(bf16[2048,512]{1,0:T(8,128)(2,1)} %param.5) | copy-start | bytes 6291460
  10.0 3.3 %copy-start.17 = (s32[2048]{0:T(1024)S(1)}, s32[2048]{0:T(1024)}, u32[]{:S(2)}) copy-start(s32[2048]{0:T(1024)} %param.6) | copy-start | bytes 24580
  11.7 2.7 %copy-start.11 = (f32[2048,17]{0,1:T(8,128)}, f32[2048,17]{0,1:T(8,128)S(1)}, u32[]{:S(2)}) copy-start(f32[2048,17]{0,1:T(8,128)S(1)} %fusion.11) | copy-start | bytes 417796
  13.3 1.5 copy-start.15
  23.5 64.9 %all-to-all-start = ((bf16[16,176,512]{2,1,0:T(8,128)(2,1)}), bf16[16,176,512]{2,1,0:T(8,128)(2,1)}, u32[]{:S(2)}, u32[]{:S(2)}) async-start(bf16[16,176,512]{2,1,0:T(8,128)(2,1)} %add_convert_fusion), calls=%async_computation | async-start | bytes 5767168 | tf_op jit(solution)/shard_map/all_to_all | solution.py:130
  31.8 90.8 %all-gather.5.cloned.1.call-start = ((), (), s32[]{:S(2)}) async-start(), calls=%async_computation.3 | async-start | bytes 8650752 | tf_op jit(solution)/shard_map/all_gather | solution.py:166
  32.2 56.1 %copy-start.14 = (s32[4096]{0:T(1024)S(1)}, s32[4096]{0:T(1024)}, u32[]{:S(2)}) copy-start(s32[4096]{0:T(1024)} %param.7) | copy-start | bytes 49156
  37.0 52.7 %copy-start.18 = (pred[176]{0:T(512)(128)(4,1)S(1)}, pred[176]{0:T(512)(128)(4,1)}, u32[]{:S(2)}) copy-start(pred[176]{0:T(512)(128)(4,1)} %constant.18.clone.1) | copy-start | bytes 532
  90.0 57.4 %all-to-all-start.1 = ((bf16[16,96,512]{2,1,0:T(8,128)(2,1)}), bf16[16,96,512]{2,1,0:T(8,128)(2,1)}, u32[]{:S(2)}, u32[]{:S(2)}) async-start(bf16[16,96,512]{2,1,0:T(8,128)(2,1)} %bitcast.44), calls=%async_computation.1 | async-start | bytes 3145728 | tf_op jit(solution)/shard_map/all_to_all | solution.py:132
  103.8 57.2 %all-gather.7.cloned.1.call-start = ((), (), s32[]{:S(2)}) async-start(), calls=%async_computation.4 | async-start | bytes 4718592 | tf_op jit(solution)/shard_map/all_gather | solution.py:166
  122.6 6.0 %copy-start.9 = (s32[2,2816]{1,0:T(2,128)}, s32[2,2816]{1,0:T(2,128)S(1)}, u32[]{:S(2)}) copy-start(s32[2,2816]{1,0:T(2,128)S(1)} %pad_add_fusion.refs_3_) | copy-start | bytes 67588
  128.5 2.6 %copy-start.1 = (bf16[32,176,512]{2,1,0:T(8,128)(2,1)S(1)}, bf16[32,176,512]{2,1,0:T(8,128)(2,1)}, u32[]{:S(2)}) copy-start(bf16[32,176,512]{2,1,0:T(8,128)(2,1)} %all-gather.5.cloned.1.call-done) | copy-start | bytes 17301508
  145.1 1.5 copy-start.5
  161.0 2.8 %copy-start.3 = (bf16[32,96,512]{2,1,0:T(8,128)(2,1)S(1)}, bf16[32,96,512]{2,1,0:T(8,128)(2,1)}, u32[]{:S(2)}) copy-start(bf16[32,96,512]{2,1,0:T(8,128)(2,1)} %all-gather.7.cloned.1.call-done) | copy-start | bytes 9437188
  165.1 10.1 %copy-start.13 = (f32[16,96]{1,0:T(8,128)}, f32[16,96]{1,0:T(8,128)S(1)}, u32[]{:S(2)}) copy-start(f32[16,96]{1,0:T(8,128)S(1)} %add_rsqrt_fusion.1) | copy-start | bytes 18436
  165.2 1.9 copy-start.4
  167.0 1.7 copy-start.6
  168.8 6.4 %copy-start.7 = (bf16[2,16,48,512]{3,2,1,0:T(8,128)(2,1)S(1)}, bf16[2,16,48,512]{3,2,1,0:T(8,128)(2,1)}, u32[]{:S(2)}) copy-start(bf16[2,16,48,512]{3,2,1,0:T(8,128)(2,1)} %constant_dynamic-slice_fusion.1) | copy-start | bytes 4718596
  168.8 6.4 %copy-start.8 = (s32[768,2]{1,0:T(8,128)S(1)}, s32[768,2]{1,0:T(8,128)}, u32[]{:S(2)}) copy-start(s32[768,2]{1,0:T(8,128)} %copy.15.refs_2_) | copy-start | bytes 18436
  175.2 4.9 %copy-start.10 = (s32[2,2816]{1,0:T(2,128)S(1)}, s32[2,2816]{1,0:T(2,128)}, u32[]{:S(2)}) copy-start(s32[2,2816]{1,0:T(2,128)} %copy-done.9) | copy-start | bytes 67588
  180.2 2.6 %copy-start.2 = (bf16[32,176,512]{2,1,0:T(8,128)(2,1)S(1)}, bf16[32,176,512]{2,1,0:T(8,128)(2,1)}, u32[]{:S(2)}) copy-start(bf16[32,176,512]{2,1,0:T(8,128)(2,1)} %all-gather.5.cloned.1.call-done) | copy-start | bytes 17301508
  196.3 17.7 %all-to-all-start.2 = ((f32[32,1,128]{2,1,0:T(1,128)}), f32[32,1,128]{2,1,0:T(1,128)S(1)}, u32[]{:S(2)}, u32[]{:S(2)}) async-start(f32[32,1,128]{2,1,0:T(1,128)} %bitcast.11), calls=%async_computation.2 | async-start | bytes 32768 | tf_op jit(solution)/shard_map/all_to_all | solution.py:194
  202.3 11.9 %copy-start.12 = (f32[2048,17]{0,1:T(8,128)S(1)}, f32[2048,17]{0,1:T(8,128)}, u32[]{:S(2)}) copy-start(f32[2048,17]{0,1:T(8,128)} %copy-done.11) | copy-start | bytes 417796
  202.3 11.9 %copy-start.16 = (s32[2048]{0:T(1024)S(1)}, s32[2048]{0:T(1024)}, u32[]{:S(2)}) copy-start(s32[2048]{0:T(1024)} %copy-done.15) | copy-start | bytes 24580
Sparse Core Ops, SparseCore 0:
  88.5 24.0 all-gather.4
  147.6 13.3 all-gather.6

commit v3 on v2

--- a/solution.py
+++ b/solution.py
@@ -46,7 +46,7 @@
 def gram_best(diagonal, own, every, key_i, key_j, inv_j):
     parts, rows, half = own.shape
     cols = every.shape[1]
-    ti, tj = tile(rows, 16, 640), tile(cols, 128, 512)
+    ti, tj = tile(rows, 16, 448), tile(cols, 128, 512)
     out = pl.pallas_call(
         lambda *refs: gram_kernel(diagonal, *refs),
         grid=(rows // ti, cols // tj),
@@ -60,7 +60,7 @@
         out_specs=pl.BlockSpec((ti, 1), lambda i, j: (i, 0)),
         out_shape=jax.ShapeDtypeStruct((rows, 1), jnp.float32),
         scratch_shapes=[pltpu.VMEM((ti, 128), jnp.float32)],
-        compiler_params=pltpu.CompilerParams(vmem_limit_bytes=40 * 1024 * 1024),
+        compiler_params=pltpu.CompilerParams(vmem_limit_bytes=56 * 1024 * 1024),
         cost_estimate=pl.CostEstimate(
             flops=2 * rows * cols * parts * half,
             bytes_accessed=2 * parts * half * (rows + cols * (rows // ti)),
@@ -87,7 +87,7 @@
     cap = 2 * doc_rows // n_dp
     owned = old_centroids.shape[0]
     n_blocks = block_owner.shape[0]
-    first = cap * 5 // 8
+    first = -(-(cap * 7 // 16) // n_grp) * n_grp
     starts, widths = (0, first), (first, cap - first)
     heights = (first + EXTRA, cap - first)
 
@@ -164,6 +164,9 @@
         hot = (jnp.arange(owned, dtype=jnp.int32)[:, None] == line[None, :]).astype(BF)
         total = total + dot(hot, got[c].reshape(part_rows, half))
         every = lax.all_gather(got[c], "group", axis=0)
+        if c:
+            total = total / (prev + counts)[:, None]
+        total, every = lax.optimization_barrier((total, every))
         own = own_part(every, 2).reshape(n_grp, n_dp * mine, half)
         every = every.reshape(n_grp, part_rows, half)
         squares = jnp.sum(jnp.square(every.astype(jnp.float32)), axis=(0, 2))
@@ -202,8 +205,7 @@
     )
     max_sim = jnp.sum(jnp.where(order_hot, rows, 0.0), axis=1)
     max_sim = jnp.where(valid, max_sim, -1.0)
-    new_centroids = total / (prev + counts)[:, None]
-    return (new_centroids, max_sim)
+    return (total, max_sim)
 
 
 def solution(mesh):

time: 224 us -> 231 us (1.031)
  Pallas kernels: 35.9 us -> 56.4 us
  blocking collectives: 0 us -> 13.9 us
  starting transfers between devices: 28.4 us -> 18.6 us
  local copies, waits for them, and re-layouts: 19.1 us -> 9.63 us
  waiting for transfers between devices: 60.6 us -> 51.3 us
    pallas_call x4, Pallas kernels: 35.9 us -> 56.4 us  [gram_best(): pl.pallas_call(lambda *refs: gram_kernel(diagonal, *refs), grid=(rows //...]
    all_to_all x1, waiting for transfers between devices: 51.3 us -> 36 us  [on_device(): lax.all_to_all(outgoing[0], 'dp', split_axis=0, concat_axis=0, tiled=True)]
    all_to_all x0 -> x1, blocking collectives: none -> 13.9 us  [on_device(): lax.all_to_all(spread, ('dp', 'group'), split_axis=0, concat_axis=0, tile...]
    all_to_all x1, waiting for transfers between devices: 0.01 us -> 12.5 us  [on_device(): lax.all_to_all(later, 'dp', split_axis=0, concat_axis=0, tiled=True)]
    unnamed x42 -> x20, local copies, waits for them, and re-layouts: 11.2 us -> 0.91 us
    all_gather x2, waiting for transfers between devices: 9.19 us -> 2.83 us  [on_device(): every = lax.all_gather(got[c], 'group', axis=0)]
    all_to_all x1 -> x0, starting transfers between devices: 5.99 us -> none  [on_device(): lax.all_to_all(spread, ('dp', 'group'), split_axis=0, concat_axis=0, tile...]
    all_to_all x1, starting transfers between devices: 13.8 us -> 10 us  [on_device(): lax.all_to_all(later, 'dp', split_axis=0, concat_axis=0, tiled=True)]
  transfers between devices with their start and end apart: 5 -> 4, of which waited for: 2 -> 3; matrix products, arithmetic and copies ran while one was open for 21% -> 22% of each run, Pallas kernels for 6% -> 5%
where the time goes in v3:
time: 231 us; the launch traced here: 230 us
  Pallas kernels  56.4 us (24%)
  waiting for transfers between devices  51.3 us (22%)
  matrix products  48.2 us (21%)
  starting transfers between devices  18.6 us (8%)
  other arithmetic  17.1 us (7%)
  between operations  14.5 us (6%)
  blocking collectives  13.9 us (6%)
  local copies, waits for them, and re-layouts  9.63 us (4%)
    pallas_call x4, Pallas kernels, gram_best(): pl.pallas_call(lambda *refs: gram_kernel(diagonal, *refs), grid=(rows //...  56.4 us
    dot_general x8, matrix products, dot(): return jnp.dot(a, b, preferred_element_type=jnp.float32)  45.5 us
    all_to_all x1, waiting for transfers between devices, on_device(): lax.all_to_all(outgoing[0], 'dp', split_axis=0, concat_axis=0, tiled=True)  36 us
    all_to_all x1, blocking collectives, on_device(): lax.all_to_all(spread, ('dp', 'group'), split_axis=0, concat_axis=0, tile...  13.9 us
    all_to_all x1, waiting for transfers between devices, on_device(): lax.all_to_all(later, 'dp', split_axis=0, concat_axis=0, tiled=True)  12.5 us
    all_to_all x1, starting transfers between devices, on_device(): lax.all_to_all(later, 'dp', split_axis=0, concat_axis=0, tiled=True)  10 us
    all_to_all x1, starting transfers between devices, on_device(): lax.all_to_all(outgoing[0], 'dp', split_axis=0, concat_axis=0, tiled=True)  8.36 us
    reduce_sum x2, other arithmetic, on_device(): squares = jnp.sum(jnp.square(every.astype(jnp.float32)), axis=(0, 2))  6.6 us
  transfers between devices with their start and end apart: 4, of which 3 were waited for; matrix products, arithmetic and copies ran while one was open for 22% of the time, Pallas kernels for 5%

profile of v3, /device:TPU:0, one launch (start us, length us, event | category | flops | bytes accessed | tf_op | source)
XLA Modules:
  0.0 229.7 jit_solution(14671131213159833699)
XLA Ops:
  7.2 0.8 fusion.35
  8.0 1.3 fusion.28
  9.3 0.7 broadcast_shift-right-arithmetic_fusion
  10.0 1.7 fusion.13
  11.7 1.5 fusion.26
  13.2 0.1 multiply_reduce_fusion.2
  13.3 0.4 select_convert_fusion.1
  13.8 0.6 fusion.20
  14.5 0.3 copy.17
  14.8 0.1 select_bitcast_fusion
  14.9 4.7 %fusion.6 = f32[2048,512]{1,0:T(8,128)S(1)} fusion(bf16[2048,512]{1,0:T(8,128)(2,1)S(1)} %copy-done, s32[2048]{0:T(1024)S(1)} %get-tuple-element.22, s32[2048]{0:T(1024)S(1)} %select_bitcast_fusion), kind=kOutput, calls=%fused_computation.9 | convolution fusion | flops 4299161600 | bytes 6307840 | tf_op jit(solution)/shard_map/dot_general | solution.py:79
  19.6 1.6 add_convert_fusion
  21.2 8.4 %all-to-all-start = ((bf16[16,128,512]{2,1,0:T(8,128)(2,1)}), bf16[16,128,512]{2,1,0:T(8,128)(2,1)}, u32[]{:S(2)}, u32[]{:S(2)}) async-start(bf16[16,128,512]{2,1,0:T(8,128)(2,1)} %add_convert_fusion), calls=%async_computation | async-start | bytes 4194304 | tf_op jit(solution)/shard_map/all_to_all | solution.py:130
  29.6 0.2 all-gather.5.cloned.1.call-start
  29.8 0.1 add_select_fusion
  29.9 0.1 select_n.102
  30.0 6.7 %fusion.14 = bf16[2304,512]{1,0:T(8,128)(2,1)} fusion(bf16[2048,512]{1,0:T(8,128)(2,1)S(1)} %copy-done, s32[2048]{0:T(1024)S(1)} %get-tuple-element.22, s32[2304]{0:T(1024)S(1)} %select_n.102), kind=kOutput, calls=%fused_computation.22 | convolution fusion | flops 4837736448 | bytes 4473856 | tf_op jit(solution)/shard_map/dot_general | solution.py:79
  36.7 36.0 %all-to-all-done = bf16[16,128,512]{2,1,0:T(8,128)(2,1)} async-done(((bf16[16,128,512]{2,1,0:T(8,128)(2,1)}), bf16[16,128,512]{2,1,0:T(8,128)(2,1)}, u32[]{:S(2)}, u32[]{:S(2)}) %all-to-all-start) | async-done | bytes 2097184 | tf_op jit(solution)/shard_map/all_to_all | solution.py:130
  72.7 1.0 convert_convert_fusion
  73.8 0.3 copy.18
  74.2 0.1 eq.141
  74.3 0.1 reshape.323
  74.4 0.8 fusion.24
  75.2 0.1 reshape.321
  75.3 10.0 %all-to-all-start.1 = ((bf16[16,144,512]{2,1,0:T(8,128)(2,1)}), bf16[16,144,512]{2,1,0:T(8,128)(2,1)}, u32[]{:S(2)}, u32[]{:S(2)}) async-start(bf16[16,144,512]{2,1,0:T(8,128)(2,1)} %bitcast.43), calls=%async_computation.1 | async-start | bytes 4718592 | tf_op jit(solution)/shard_map/all_to_all | solution.py:132
  85.4 0.1 add_add_fusion.1
  85.4 0.1 reshape.315
  85.5 0.1 stack_reshape.6
  85.7 1.0 copy.13.refs_2_
  86.6 0.1 add_add_fusion
  86.7 0.1 reshape.327
  86.8 0.1 stack_reshape.7
  86.9 0.6 pad_add_fusion.1.refs_3_
  87.5 14.0 %multiply_add_fusion = f32[4096,512]{1,0:T(8,128)} fusion(f32[4096,512]{1,0:T(8,128)} %param.8, bf16[2048,512]{1,0:T(8,128)(2,1)} %bitcast.5, s32[2048]{0:T(1024)S(1)} %get-tuple-element.25, f32[4096]{0:T(1024)S(1)} %convert_element_type.91), kind=kOutput, calls=%fused_computation.19 | convolution fusion | flops 8602517504 | bytes 18898944 | tf_op jit(solution)/shard_map/dot_general | solution.py:79
  101.6 2.9 %constant_dynamic-slice_fusion.4 = bf16[2,16,56,512]{3,2,1,0:T(8,128)(2,1)} fusion(bf16[2,16,128,512]{3,2,1,0:T(8,128)(2,1)} %bitcast.38, s32[]{:T(128)S(6)} %select_n.103), kind=kLoop, calls=%fused_computation.97 | loop fusion | bytes 3670020 | tf_op jit(solution)/shard_map/dynamic_slice | solution.py:159
  104.5 3.1 %multiply_reduce_fusion.1 = f32[16,128]{1,0:T(8,128)S(1)} fusion(bf16[2,16,128,512]{3,2,1,0:T(8,128)(2,1)} %bitcast.39), kind=kLoop, calls=%fused_computation.16 | loop fusion | flops 6289408 | bytes 4202496 | tf_op jit(solution)/shard_map/reduce_sum | solution.py:172
  107.6 0.6 add_rsqrt_fusion.1
  108.2 10.4 %shard_map.68 = f32[896,1]{1,0:T(8,128)} custom-call(bf16[2,896,512]{2,1,0:T(8,128)(2,1)} %bitcast.49, bf16[2,2048,512]{2,1,0:T(8,128)(2,1)} %bitcast.40, s32[896,2]{1,0:T(8,128)} %copy.13.refs_2_, s32[2,2048]{1,0:T(2,128)} %pad_add_fusion.1.refs_3_, f32[1,2048]{1,0:T(1,128)} %bitcast.57), custom_call_target="tpu_custom_call" | custom-call | flops 3758096384 | bytes 10223616 | tf_op jit(solution)/shard_map/pallas_call | solution.py:50
  118.6 1.2 reduce.2
  119.8 12.5 %all-to-all-done.1 = bf16[16,144,512]{2,1,0:T(8,128)(2,1)} async-done(((bf16[16,144,512]{2,1,0:T(8,128)(2,1)}), bf16[16,144,512]{2,1,0:T(8,128)(2,1)}, u32[]{:S(2)}, u32[]{:S(2)}) %all-to-all-start.1) | async-done | bytes 2359328 | tf_op jit(solution)/shard_map/all_to_all | solution.py:132
  132.4 1.1 copy.15.refs_2_
  133.5 0.6 pad_add_fusion.refs_3_
  134.2 0.1 reshape.324
  134.3 15.0 %add_divide_fusion = f32[4096,512]{1,0:T(8,128)} fusion(f32[4096,512]{1,0:T(8,128)} %multiply_add_fusion, bf16[2304,512]{1,0:T(8,128)(2,1)} %bitcast.11, s32[2304]{0:T(1024)S(1)} %eq.141, f32[4096]{0:T(1024)S(1)} %convert_add_fusion), kind=kOutput, calls=%fused_computation.15 | convolution fusion | flops 9677307904 | bytes 19162112 | tf_op jit(solution)/shard_map/dot_general | solution.py:79
  149.3 2.8 %all-gather.7.cloned.1.call-done = bf16[32,144,512]{2,1,0:T(8,128)(2,1)} async-done(((bf16[16,144,512]{2,1,0:T(8,128)(2,1)}), bf16[32,144,512]{2,1,0:T(8,128)(2,1)}) %all-gather.7.cloned.1.call-update) | async-done | bytes 4718608 | tf_op jit(solution)/shard_map/all_gather | solution.py:166
  152.1 3.5 %multiply_reduce_fusion = f32[16,144]{1,0:T(8,128)S(1)} fusion(bf16[2,16,144,512]{3,2,1,0:T(8,128)(2,1)} %bitcast.34), kind=kLoop, calls=%fused_computation.12 | loop fusion | flops 7075584 | bytes 4727808 | tf_op jit(solution)/shard_map/reduce_sum | solution.py:172
  155.6 0.2 copy-done.1
  155.9 1.6 constant_dynamic-slice_fusion.1
  157.5 0.7 rsqrt.31.refs_4_
  158.2 13.4 %shard_map.69 = f32[896,1]{1,0:T(8,128)} custom-call(bf16[2,896,512]{2,1,0:T(8,128)(2,1)} %bitcast.50, bf16[2,2304,512]{2,1,0:T(8,128)(2,1)} %bitcast.35, s32[896,2]{1,0:T(8,128)} %copy.13.refs_2_, s32[2,2304]{1,0:T(2,128)} %pad_add_fusion.refs_3_, f32[1,2304]{1,0:T(1,128)} %rsqrt.31.refs_4_), custom_call_target="tpu_custom_call" | custom-call | flops 4227858432 | bytes 11272192 | tf_op jit(solution)/shard_map/pallas_call | solution.py:50
  171.6 18.6 %shard_map.71 = f32[1152,1]{1,0:T(8,128)} custom-call(bf16[2,1152,512]{2,1,0:T(8,128)(2,1)} %bitcast.44, bf16[2,2304,512]{2,1,0:T(8,128)(2,1)} %bitcast.36, s32[1152,2]{1,0:T(8,128)} %copy.15.refs_2_, s32[2,2304]{1,0:T(2,128)} %pad_add_fusion.refs_3_, f32[1,2304]{1,0:T(1,128)} %rsqrt.31.refs_4_), custom_call_target="tpu_custom_call" | custom-call | flops 5435817984 | bytes 16515072 | tf_op jit(solution)/shard_map/pallas_call | solution.py:50
  190.2 13.9 %shard_map.70 = f32[1152,1]{1,0:T(8,128)} custom-call(bf16[2,1152,512]{2,1,0:T(8,128)(2,1)} %bitcast.45, bf16[2,2048,512]{2,1,0:T(8,128)(2,1)} %bitcast.41, s32[1152,2]{1,0:T(8,128)} %copy.15.refs_2_, s32[2,2048]{1,0:T(2,128)} %pad_add_fusion.1.refs_3_, f32[1,2048]{1,0:T(1,128)} %bitcast.58), custom_call_target="tpu_custom_call" | custom-call | flops 4831838208 | bytes 14942208 | tf_op jit(solution)/shard_map/pallas_call | solution.py:50
  204.1 0.2 reduce.3
  204.4 0.1 reshape.325
  204.5 1.3 maximum_reduce_fusion
  205.8 0.1 max.27
  205.9 0.1 multiply_maximum_fusion
  205.9 0.1 pad_maximum_fusion
  206.0 13.9 %all_to_all.19 = f32[32,1,128]{2,1,0:T(1,128)S(1)} all-to-all(f32[32,1,128]{2,1,0:T(1,128)S(1)} %bitcast.55), channel_id=1, replica_groups=mesh['dp'=16,'group'=2] {'dp','group'}, dimensions={0} | all-to-all | bytes 32768 | tf_op jit(solution)/shard_map/all_to_all | solution.py:197
  219.9 0.1 slice.44
  220.0 0.1 reshape.333
  220.1 0.1 reshape.332
  220.2 2.0 fusion.25
  222.2 0.6 broadcast_select_fusion
  (51 shorter events, 0.5 us)
Async XLA Ops:
  7.2 7.7 %copy-start = (bf16[2048,512]{1,0:T(8,128)(2,1)S(1)}, bf16[2048,512]{1,0:T(8,128)(2,1)}, u32[]{:S(2)}) copy-start(bf16[2048,512]{1,0:T(8,128)(2,1)} %param.5) | copy-start | bytes 6291460
  10.0 3.3 %copy-start.5 = (s32[2048]{0:T(1024)S(1)}, s32[2048]{0:T(1024)}, u32[]{:S(2)}) copy-start(s32[2048]{0:T(1024)} %param.6) | copy-start | bytes 24580
  19.6 10.5 %copy-start.4 = (s32[4096]{0:T(1024)S(1)}, s32[4096]{0:T(1024)}, u32[]{:S(2)}) copy-start(s32[4096]{0:T(1024)} %param.7) | copy-start | bytes 49156
  21.2 51.5 %all-to-all-start = ((bf16[16,128,512]{2,1,0:T(8,128)(2,1)}), bf16[16,128,512]{2,1,0:T(8,128)(2,1)}, u32[]{:S(2)}, u32[]{:S(2)}) async-start(bf16[16,128,512]{2,1,0:T(8,128)(2,1)} %add_convert_fusion), calls=%async_computation | async-start | bytes 4194304 | tf_op jit(solution)/shard_map/all_to_all | solution.py:130
  29.6 72.0 %all-gather.5.cloned.1.call-start = ((), (), s32[]{:S(2)}) async-start(), calls=%async_computation.3 | async-start | bytes 6291456 | tf_op jit(solution)/shard_map/all_gather | solution.py:166
  72.7 12.6 %copy-start.7 = (pred[128]{0:T(512)(128)(4,1)S(1)}, pred[128]{0:T(512)(128)(4,1)}, u32[]{:S(2)}) copy-start(pred[128]{0:T(512)(128)(4,1)} %constant.18.clone.1) | copy-start | bytes 388
  75.3 57.0 %all-to-all-start.1 = ((bf16[16,144,512]{2,1,0:T(8,128)(2,1)}), bf16[16,144,512]{2,1,0:T(8,128)(2,1)}, u32[]{:S(2)}, u32[]{:S(2)}) async-start(bf16[16,144,512]{2,1,0:T(8,128)(2,1)} %bitcast.43), calls=%async_computation.1 | async-start | bytes 4718592 | tf_op jit(solution)/shard_map/all_to_all | solution.py:132
  85.3 66.8 %all-gather.7.cloned.1.call-start = ((), (), s32[]{:S(2)}) async-start(), calls=%async_computation.4 | async-start | bytes 7077888 | tf_op jit(solution)/shard_map/all_gather | solution.py:166
  108.2 26.0 %copy-start.6 = (f32[16,128]{1,0:T(8,128)S(1)}, f32[16,128]{1,0:T(8,128)}, u32[]{:S(2)}) copy-start(f32[16,128]{1,0:T(8,128)} %add_rsqrt_fusion.1) | copy-start | bytes 24580
  152.1 3.8 %copy-start.1 = (bf16[32,144,512]{2,1,0:T(8,128)(2,1)S(1)}, bf16[32,144,512]{2,1,0:T(8,128)(2,1)}, u32[]{:S(2)}) copy-start(bf16[32,144,512]{2,1,0:T(8,128)(2,1)} %all-gather.7.cloned.1.call-done) | copy-start | bytes 14155780
  190.2 13.9 %copy-start.3 = (f32[896,1]{1,0:T(8,128)S(1)}, f32[896,1]{1,0:T(8,128)}, u32[]{:S(2)}) copy-start(f32[896,1]{1,0:T(8,128)} %shard_map.69) | copy-start | bytes 10756
  190.2 14.2 %copy-start.2 = (f32[1152,1]{1,0:T(8,128)S(1)}, f32[1152,1]{1,0:T(8,128)}, u32[]{:S(2)}) copy-start(f32[1152,1]{1,0:T(8,128)} %shard_map.71) | copy-start | bytes 13828
Sparse Core Ops, SparseCore 0:
  72.8 18.0 all-gather.4
  132.4 19.6 all-gather.6

commit v4 on v3

--- a/solution.py
+++ b/solution.py
@@ -46,7 +46,7 @@
 def gram_best(diagonal, own, every, key_i, key_j, inv_j):
     parts, rows, half = own.shape
     cols = every.shape[1]
-    ti, tj = tile(rows, 16, 448), tile(cols, 128, 512)
+    ti, tj = tile(rows, 128, 640), tile(cols, 256, 512)
     out = pl.pallas_call(
         lambda *refs: gram_kernel(diagonal, *refs),
         grid=(rows // ti, cols // tj),
@@ -60,7 +60,7 @@
         out_specs=pl.BlockSpec((ti, 1), lambda i, j: (i, 0)),
         out_shape=jax.ShapeDtypeStruct((rows, 1), jnp.float32),
         scratch_shapes=[pltpu.VMEM((ti, 128), jnp.float32)],
-        compiler_params=pltpu.CompilerParams(vmem_limit_bytes=56 * 1024 * 1024),
+        compiler_params=pltpu.CompilerParams(vmem_limit_bytes=min(56, 32 + 4 * parts) * 1024 * 1024),
         cost_estimate=pl.CostEstimate(
             flops=2 * rows * cols * parts * half,
             bytes_accessed=2 * parts * half * (rows + cols * (rows // ti)),
@@ -87,7 +87,7 @@
     cap = 2 * doc_rows // n_dp
     owned = old_centroids.shape[0]
     n_blocks = block_owner.shape[0]
-    first = -(-(cap * 7 // 16) // n_grp) * n_grp
+    first = -(-(cap // 2) // n_grp) * n_grp
     starts, widths = (0, first), (first, cap - first)
     heights = (first + EXTRA, cap - first)
 

time: 231 us -> 208 us (0.900)
  Pallas kernels: 56.4 us -> 35.6 us
  other arithmetic: 17.1 us -> 14.4 us
    pallas_call x4, Pallas kernels: 56.4 us -> 35.6 us  [gram_best(): pl.pallas_call(lambda *refs: gram_kernel(diagonal, *refs), grid=(rows //...]
    all_to_all x1, waiting for transfers between devices: 36 us -> 41.6 us  [on_device(): lax.all_to_all(outgoing[0], 'dp', split_axis=0, concat_axis=0, tiled=True)]
    all_to_all x1, waiting for transfers between devices: 12.5 us -> 6.9 us  [on_device(): lax.all_to_all(later, 'dp', split_axis=0, concat_axis=0, tiled=True)]
    unnamed x20 -> x28, local copies, waits for them, and re-layouts: 0.91 us -> 5.85 us
    dynamic_slice x3, local copies, waits for them, and re-layouts: 4.58 us -> 2.1 us  [own_part(): return lax.dynamic_slice_in_dim(x, grp * mine, mine, axis)]
where the time goes in v4:
time: 208 us; the launch traced here: 207 us
  waiting for transfers between devices  50.3 us (24%)
  matrix products  48.3 us (23%)
  Pallas kernels  35.6 us (17%)
  starting transfers between devices  19.8 us (10%)
  between operations  14.6 us (7%)
  other arithmetic  14.4 us (7%)
  blocking collectives  14 us (7%)
  local copies, waits for them, and re-layouts  10.5 us (5%)
    dot_general x8, matrix products, dot(): return jnp.dot(a, b, preferred_element_type=jnp.float32)  45.7 us
    all_to_all x1, waiting for transfers between devices, on_device(): lax.all_to_all(outgoing[0], 'dp', split_axis=0, concat_axis=0, tiled=True)  41.6 us
    pallas_call x4, Pallas kernels, gram_best(): pl.pallas_call(lambda *refs: gram_kernel(diagonal, *refs), grid=(rows //...  35.6 us
    all_to_all x1, blocking collectives, on_device(): lax.all_to_all(spread, ('dp', 'group'), split_axis=0, concat_axis=0, tile...  14 us
    all_to_all x1, starting transfers between devices, on_device(): lax.all_to_all(later, 'dp', split_axis=0, concat_axis=0, tiled=True)  11.1 us
    all_to_all x1, starting transfers between devices, on_device(): lax.all_to_all(outgoing[0], 'dp', split_axis=0, concat_axis=0, tiled=True)  8.49 us
    all_to_all x1, waiting for transfers between devices, on_device(): lax.all_to_all(later, 'dp', split_axis=0, concat_axis=0, tiled=True)  6.9 us
    reduce_sum x2, other arithmetic, on_device(): squares = jnp.sum(jnp.square(every.astype(jnp.float32)), axis=(0, 2))  6.6 us
  transfers between devices with their start and end apart: 4, of which 3 were waited for; matrix products, arithmetic and copies ran while one was open for 22% of the time, Pallas kernels for 5%

profile of v4, /device:TPU:0, one launch (start us, length us, event | category | flops | bytes accessed | tf_op | source)
XLA Modules:
  0.0 207.4 jit_solution(14905233770130722408)
XLA Ops:
  7.2 0.8 fusion.35
  8.0 1.3 fusion.28
  9.3 0.7 broadcast_shift-right-arithmetic_fusion
  10.0 1.7 fusion.13
  11.7 1.5 fusion.26
  13.2 0.1 multiply_reduce_fusion.2
  13.3 0.4 select_convert_fusion.1
  13.8 0.6 fusion.20
  14.5 0.3 copy.17
  14.8 0.1 add_select_fusion
  14.9 0.1 select_n.96
  15.0 5.3 %fusion.3 = f32[2304,512]{1,0:T(8,128)S(1)} fusion(bf16[2048,512]{1,0:T(8,128)(2,1)S(1)} %copy-done, s32[2048]{0:T(1024)S(1)} %get-tuple-element.22, s32[2304]{0:T(1024)S(1)} %select_n.96), kind=kOutput, calls=%fused_computation.5 | convolution fusion | flops 4836556800 | bytes 6833152 | tf_op jit(solution)/shard_map/dot_general | solution.py:79
  20.2 1.8 add_convert_fusion
  22.1 8.5 %all-to-all-start = ((bf16[16,144,512]{2,1,0:T(8,128)(2,1)}), bf16[16,144,512]{2,1,0:T(8,128)(2,1)}, u32[]{:S(2)}, u32[]{:S(2)}) async-start(bf16[16,144,512]{2,1,0:T(8,128)(2,1)} %add_convert_fusion), calls=%async_computation | async-start | bytes 4718592 | tf_op jit(solution)/shard_map/all_to_all | solution.py:130
  30.6 0.2 all-gather.5.cloned.1.call-start
  30.8 0.1 select_bitcast_fusion
  30.9 5.8 %fusion.16 = bf16[2048,512]{1,0:T(8,128)(2,1)} fusion(bf16[2048,512]{1,0:T(8,128)(2,1)S(1)} %copy-done, s32[2048]{0:T(1024)S(1)} %get-tuple-element.22, s32[2048]{0:T(1024)S(1)} %select_bitcast_fusion), kind=kOutput, calls=%fused_computation.26 | convolution fusion | flops 4300210176 | bytes 4210688 | tf_op jit(solution)/shard_map/dot_general | solution.py:79
  36.7 41.6 %all-to-all-done = bf16[16,144,512]{2,1,0:T(8,128)(2,1)} async-done(((bf16[16,144,512]{2,1,0:T(8,128)(2,1)}), bf16[16,144,512]{2,1,0:T(8,128)(2,1)}, u32[]{:S(2)}, u32[]{:S(2)}) %all-to-all-start) | async-done | bytes 2359328 | tf_op jit(solution)/shard_map/all_to_all | solution.py:130
  78.3 1.0 convert_convert_fusion
  79.3 0.3 copy.18
  79.7 0.1 reshape.319
  79.8 0.1 add_add_fusion.1
  79.8 0.1 reshape.315
  79.9 0.1 stack_reshape.6
  80.0 11.1 %all-to-all-start.1 = ((bf16[16,128,512]{2,1,0:T(8,128)(2,1)}), bf16[16,128,512]{2,1,0:T(8,128)(2,1)}, u32[]{:S(2)}, u32[]{:S(2)}) async-start(bf16[16,128,512]{2,1,0:T(8,128)(2,1)} %bitcast.51), calls=%async_computation.1 | async-start | bytes 4194304 | tf_op jit(solution)/shard_map/all_to_all | solution.py:132
  91.2 0.1 eq.137
  91.3 0.2 copy.13.refs_2_
  91.5 15.7 %multiply_add_fusion = f32[4096,512]{1,0:T(8,128)} fusion(f32[4096,512]{1,0:T(8,128)} %param.8, bf16[2304,512]{1,0:T(8,128)(2,1)} %bitcast.4, s32[2304]{0:T(1024)S(1)} %eq.137, f32[4096]{0:T(1024)S(1)} %convert_element_type.91), kind=kOutput, calls=%fused_computation.19 | convolution fusion | flops 9677307904 | bytes 19162112 | tf_op jit(solution)/shard_map/dot_general | solution.py:79
  107.2 3.4 %multiply_reduce_fusion = f32[16,144]{1,0:T(8,128)S(1)} fusion(bf16[2,16,144,512]{3,2,1,0:T(8,128)(2,1)} %bitcast.33), kind=kLoop, calls=%fused_computation.12 | loop fusion | flops 7075584 | bytes 4727808 | tf_op jit(solution)/shard_map/reduce_sum | solution.py:172
  110.6 0.1 rsqrt.29.refs_4_
  110.7 1.8 constant_dynamic-slice_fusion.4
  112.5 2.3 %copy-done.1 = bf16[32,144,512]{2,1,0:T(8,128)(2,1)S(1)} copy-done((bf16[32,144,512]{2,1,0:T(8,128)(2,1)S(1)}, bf16[32,144,512]{2,1,0:T(8,128)(2,1)}, u32[]{:S(2)}) %copy-start.1) | copy-done | bytes 4718616
  114.9 10.3 %shard_map.68 = f32[1024,1]{1,0:T(8,128)S(1)} custom-call(bf16[2,1024,512]{2,1,0:T(8,128)(2,1)S(1)} %bitcast.43, bf16[2,2304,512]{2,1,0:T(8,128)(2,1)S(1)} %bitcast.35, s32[1024,2]{1,0:T(8,128)S(1)} %copy.13.refs_2_, s32[2,2304]{1,0:T(2,128)S(1)} %pad_add_fusion.refs_3_, f32[1,2304]{1,0:T(1,128)S(1)} %rsqrt.29.refs_4_), custom_call_target="tpu_custom_call" | custom-call | flops 4831838208 | bytes 11534336 | tf_op jit(solution)/shard_map/pallas_call | solution.py:50
  125.2 1.4 copy-done.3
  126.6 0.2 reduce.2
  126.8 6.9 %all-to-all-done.1 = bf16[16,128,512]{2,1,0:T(8,128)(2,1)} async-done(((bf16[16,128,512]{2,1,0:T(8,128)(2,1)}), bf16[16,128,512]{2,1,0:T(8,128)(2,1)}, u32[]{:S(2)}, u32[]{:S(2)}) %all-to-all-start.1) | async-done | bytes 2097184 | tf_op jit(solution)/shard_map/all_to_all | solution.py:132
  133.8 0.8 fusion.24
  134.5 0.1 reshape.321
  134.6 0.1 add_add_fusion
  134.7 0.1 reshape.327
  134.7 0.1 stack_reshape.7
  134.9 1.1 copy.15.refs_2_
  136.0 0.1 constant_dynamic-slice_fusion.2
  136.1 0.1 reshape.324
  136.1 13.8 %add_divide_fusion = f32[4096,512]{1,0:T(8,128)} fusion(f32[4096,512]{1,0:T(8,128)} %multiply_add_fusion, bf16[2048,512]{1,0:T(8,128)(2,1)} %bitcast.9, s32[2048]{0:T(1024)S(1)} %get-tuple-element.27, f32[4096]{0:T(1024)S(1)} %convert_add_fusion), kind=kOutput, calls=%fused_computation.16 | convolution fusion | flops 8602517504 | bytes 18898944 | tf_op jit(solution)/shard_map/dot_general | solution.py:79
  149.9 1.8 all-gather.7.cloned.1.call-done
  151.7 3.2 %multiply_reduce_fusion.1 = f32[16,128]{1,0:T(8,128)S(1)} fusion(bf16[2,16,128,512]{3,2,1,0:T(8,128)(2,1)} %bitcast.39), kind=kLoop, calls=%fused_computation.15 | loop fusion | flops 6289408 | bytes 4202496 | tf_op jit(solution)/shard_map/reduce_sum | solution.py:172
  154.9 0.2 copy-done.2
  155.2 0.2 constant_dynamic-slice_fusion.1
  155.4 0.5 copy-done.4
  155.8 7.2 %shard_map.69 = f32[1024,1]{1,0:T(8,128)S(1)} custom-call(bf16[2,1024,512]{2,1,0:T(8,128)(2,1)S(1)} %bitcast.44, bf16[2,2048,512]{2,1,0:T(8,128)(2,1)S(1)} %bitcast.41, s32[1024,2]{1,0:T(8,128)S(1)} %copy.13.refs_2_, s32[2,2048]{1,0:T(2,128)S(1)} %pad_add_fusion.1.refs_3_, f32[1,2048]{1,0:T(1,128)S(1)} %bitcast.47), custom_call_target="tpu_custom_call" | custom-call | flops 4294967296 | bytes 10485760 | tf_op jit(solution)/shard_map/pallas_call | solution.py:50
  163.1 7.9 %shard_map.71 = f32[1024,1]{1,0:T(8,128)S(1)} custom-call(bf16[2,1024,512]{2,1,0:T(8,128)(2,1)S(1)} %bitcast.45, bf16[2,2048,512]{2,1,0:T(8,128)(2,1)S(1)} %bitcast.42, s32[1024,2]{1,0:T(8,128)S(1)} %copy-done.5, s32[2,2048]{1,0:T(2,128)S(1)} %pad_add_fusion.1.refs_3_, f32[1,2048]{1,0:T(1,128)S(1)} %bitcast.48), custom_call_target="tpu_custom_call" | custom-call | flops 4294967296 | bytes 10485760 | tf_op jit(solution)/shard_map/pallas_call | solution.py:50
  171.0 10.2 %shard_map.70 = f32[1024,1]{1,0:T(8,128)S(1)} custom-call(bf16[2,1024,512]{2,1,0:T(8,128)(2,1)S(1)} %bitcast.46, bf16[2,2304,512]{2,1,0:T(8,128)(2,1)S(1)} %bitcast.38, s32[1024,2]{1,0:T(8,128)S(1)} %copy-done.5, s32[2,2304]{1,0:T(2,128)S(1)} %pad_add_fusion.refs_3_, f32[1,2304]{1,0:T(1,128)S(1)} %rsqrt.29.refs_4_), custom_call_target="tpu_custom_call" | custom-call | flops 4831838208 | bytes 11534336 | tf_op jit(solution)/shard_map/pallas_call | solution.py:50
  181.2 0.8 copy-done.6
  182.0 0.2 reduce.3
  182.3 1.3 maximum_reduce_fusion
  183.6 0.1 multiply_maximum_fusion
  183.7 0.1 pad_maximum_fusion
  183.8 14.0 %all_to_all.19 = f32[32,1,128]{2,1,0:T(1,128)S(1)} all-to-all(f32[32,1,128]{2,1,0:T(1,128)S(1)} %bitcast.57), channel_id=1, replica_groups=mesh['dp'=16,'group'=2] {'dp','group'}, dimensions={0} | all-to-all | bytes 32768 | tf_op jit(solution)/shard_map/all_to_all | solution.py:197
  197.8 0.1 fusion.47
  197.9 0.1 reshape.332
  197.9 0.1 reshape.333
  198.0 2.0 fusion.25
  200.0 0.6 broadcast_select_fusion
  (60 shorter events, 0.6 us)
Async XLA Ops:
  7.2 7.8 %copy-start = (bf16[2048,512]{1,0:T(8,128)(2,1)S(1)}, bf16[2048,512]{1,0:T(8,128)(2,1)}, u32[]{:S(2)}) copy-start(bf16[2048,512]{1,0:T(8,128)(2,1)} %param.5) | copy-start | bytes 6291460
  10.0 3.3 %copy-start.8 = (s32[2048]{0:T(1024)S(1)}, s32[2048]{0:T(1024)}, u32[]{:S(2)}) copy-start(s32[2048]{0:T(1024)} %param.6) | copy-start | bytes 24580
  22.1 8.7 %copy-start.7 = (s32[4096]{0:T(1024)S(1)}, s32[4096]{0:T(1024)}, u32[]{:S(2)}) copy-start(s32[4096]{0:T(1024)} %param.7) | copy-start | bytes 49156
  22.1 56.2 %all-to-all-start = ((bf16[16,144,512]{2,1,0:T(8,128)(2,1)}), bf16[16,144,512]{2,1,0:T(8,128)(2,1)}, u32[]{:S(2)}, u32[]{:S(2)}) async-start(bf16[16,144,512]{2,1,0:T(8,128)(2,1)} %add_convert_fusion), calls=%async_computation | async-start | bytes 4718592 | tf_op jit(solution)/shard_map/all_to_all | solution.py:130
  30.6 76.7 %all-gather.5.cloned.1.call-start = ((), (), s32[]{:S(2)}) async-start(), calls=%async_computation.3 | async-start | bytes 7077888 | tf_op jit(solution)/shard_map/all_gather | solution.py:166
  36.7 43.0 %copy-start.9 = (pred[144]{0:T(512)(128)(4,1)S(1)}, pred[144]{0:T(512)(128)(4,1)}, u32[]{:S(2)}) copy-start(pred[144]{0:T(512)(128)(4,1)} %constant.15.clone.1) | copy-start | bytes 436
  80.0 53.7 %all-to-all-start.1 = ((bf16[16,128,512]{2,1,0:T(8,128)(2,1)}), bf16[16,128,512]{2,1,0:T(8,128)(2,1)}, u32[]{:S(2)}, u32[]{:S(2)}) async-start(bf16[16,128,512]{2,1,0:T(8,128)(2,1)} %bitcast.51), calls=%async_computation.1 | async-start | bytes 4194304 | tf_op jit(solution)/shard_map/all_to_all | solution.py:132
  91.1 60.6 %all-gather.7.cloned.1.call-start = ((), (), s32[]{:S(2)}) async-start(), calls=%async_computation.4 | async-start | bytes 6291456 | tf_op jit(solution)/shard_map/all_gather | solution.py:166
  112.5 2.3 %copy-start.1 = (bf16[32,144,512]{2,1,0:T(8,128)(2,1)S(1)}, bf16[32,144,512]{2,1,0:T(8,128)(2,1)}, u32[]{:S(2)}) copy-start(bf16[32,144,512]{2,1,0:T(8,128)(2,1)} %all-gather.5.cloned.1.call-done) | copy-start | bytes 14155780
  125.2 1.4 copy-start.3
  151.7 3.4 %copy-start.2 = (bf16[32,128,512]{2,1,0:T(8,128)(2,1)S(1)}, bf16[32,128,512]{2,1,0:T(8,128)(2,1)}, u32[]{:S(2)}) copy-start(bf16[32,128,512]{2,1,0:T(8,128)(2,1)} %all-gather.7.cloned.1.call-done) | copy-start | bytes 12582916
  151.7 4.1 %copy-start.4 = (bf16[2,16,64,512]{3,2,1,0:T(8,128)(2,1)S(1)}, bf16[2,16,64,512]{3,2,1,0:T(8,128)(2,1)}, u32[]{:S(2)}) copy-start(bf16[2,16,64,512]{3,2,1,0:T(8,128)(2,1)} %copy-done.3) | copy-start | bytes 6291460
  155.8 7.2 %copy-start.5 = (s32[1024,2]{1,0:T(8,128)S(1)}, s32[1024,2]{1,0:T(8,128)}, u32[]{:S(2)}) copy-start(s32[1024,2]{1,0:T(8,128)} %copy.15.refs_2_) | copy-start | bytes 24580
  155.8 15.2 %slice-start = ((s8[4718592]{0:T(1024)(128)(4,1)}), s8[4194304]{0:T(1024)(128)(4,1)S(1)}, s32[]{:S(2)}) async-start(s8[4718592]{0:T(1024)(128)(4,1)} %bitcast.36), calls=%async_computation.5 | async-start | bytes 8388608
  163.0 8.0 %slice-start.1 = ((s8[4718592]{0:T(1024)(128)(4,1)}), s8[524288]{0:T(1024)(128)(4,1)S(1)}, s32[]{:S(2)}) async-start(s8[4718592]{0:T(1024)(128)(4,1)} %bitcast.36), calls=%async_computation.6 | async-start | bytes 1048576
  181.2 0.8 copy-start.6
Sparse Core Ops, SparseCore 0:
  78.4 19.8 all-gather.4
  133.8 17.8 all-gather.6
